TPU v7x, 512 devices: a whole 4x8x8 slice. The times are simulated.
512 devices in a mesh: ctx: 64 (over z, x, core), kvh: 8 (over y).
Axes of the slice: x: 4, y: 8, z: 8, core: 2. Of those that a mesh axis runs over, the one named last changes fastest.
Arguments:
- queries: bfloat16 [512, 16384], P('ctx', 'kvh'), may hold values from -120 to 120
- keys: bfloat16 [262144, 1024], P('ctx', 'kvh'), may hold values from -6 to 6
- values: bfloat16 [262144, 1024], P('ctx', 'kvh'), may hold values from -6 to 6
- block_slots: int32 [512], replicated, may hold values from 0 to 511, as said below
- selected: int32 [8, 4, 64], replicated, may hold values from 0 to 511, as said below
- out_weight: bfloat16 [16384, 16384], P('kvh', 'ctx'), may hold values from -0.046875 to 0.046875
Outputs:
- projected: float32 [512, 16384], P('kvh', 'ctx')
Inputs may be any that keep to these rules, and one draw needn't show every extreme that they name: `block_slots`: a permutation of the 512 logical blocks. selected[k, c] names 64 distinct logical blocks, block 511 always among them.
All inputs are finite; a program needn't handle non-finite values.
Results may differ from a plain program's by a relative error of at most 0.013.
Values may be sent and summed in bfloat16 or wider, within the bound.
No kernel may reach another device: no remote copies, remote signals or barrier semaphores. Data moves between devices by JAX's collectives and lax.ppermute only.
A program may use at most 64 MiB of HBM per device.

v0:
```python
import math

import jax
import jax.numpy as jnp
from jax import lax
from jax.sharding import PartitionSpec as P

DH = 128
GROUP = 16
BLKSZ = 512
QBLK = 128
QTOK = 512


NEG = -1e30


def block_pairs(block_slots, chosen, device, local_blocks):
    logical = lax.dynamic_slice_in_dim(block_slots, device * local_blocks, local_blocks)
    hit = (
        jnp.any(chosen[:, None, :] == logical[None, :, None], axis=2).reshape(-1).astype(jnp.int32)
    )
    places = jnp.cumsum(hit) - 1
    count = jnp.sum(hit)
    width = hit.shape[0]
    marks = (hit[:, None] == 1) & (places[:, None] == jnp.arange(width, dtype=jnp.int32)[None, :])
    listed = jnp.sum(jnp.where(marks, jnp.arange(width, dtype=jnp.int32)[:, None], 0), axis=0)
    return (listed, count, logical)


def attend_pair(state, gathered, key_rows, value_rows, logical, pair, local_blocks, last_block):
    top, total, acc = state
    qblock = pair // local_blocks
    local = pair % local_blocks
    first = qblock * QBLK
    qrows = lax.dynamic_slice_in_dim(gathered, first, QBLK, 0).reshape(QBLK, GROUP, DH)
    kblk = lax.dynamic_slice_in_dim(key_rows, local * BLKSZ, BLKSZ, 0)
    vblk = lax.dynamic_slice_in_dim(value_rows, local * BLKSZ, BLKSZ, 0)
    block_id = logical[local]
    scores = jnp.einsum("rgd,kd->rgk", qrows, kblk, preferred_element_type=jnp.float32) * (
        1.0 / math.sqrt(DH)
    )
    qpos = BLKSZ - QTOK + first + jnp.arange(QBLK, dtype=jnp.int32)
    visible = (block_id != last_block) | (
        jnp.arange(BLKSZ, dtype=jnp.int32)[None, :] <= qpos[:, None]
    )
    scores = jnp.where(visible[:, None, :], scores, NEG)
    old_top = lax.dynamic_slice_in_dim(top, first, QBLK, 0)
    old_total = lax.dynamic_slice_in_dim(total, first, QBLK, 0)
    old_acc = lax.dynamic_slice_in_dim(acc, first, QBLK, 0)
    new_top = jnp.maximum(old_top, jnp.max(scores, axis=2))
    probs = jnp.exp(scores - new_top[:, :, None])
    fade = jnp.exp(old_top - new_top)
    new_total = old_total * fade + jnp.sum(probs, axis=2)
    weights = probs.astype(jnp.bfloat16)
    new_acc = old_acc * fade[:, :, None] + jnp.einsum(
        "rgk,kd->rgd", weights, vblk, preferred_element_type=jnp.float32
    )
    top = lax.dynamic_update_slice_in_dim(top, new_top, first, 0)
    total = lax.dynamic_update_slice_in_dim(total, new_total, first, 0)
    acc = lax.dynamic_update_slice_in_dim(acc, new_acc, first, 0)
    return (top, total, acc)


def run_list(
    state, listed, start, stop, gathered, key_rows, value_rows, logical, local_blocks, last_block
):

    def advance(index, carry):
        return attend_pair(
            carry, gathered, key_rows, value_rows, logical, listed[index], local_blocks, last_block
        )

    return lax.fori_loop(start, stop, advance, state)


def finish(received):
    top, total, acc = received
    peak = jnp.max(top, axis=0)
    weight = jnp.exp(top - peak[None])
    denom = jnp.sum(weight * total, axis=0)
    numer = jnp.sum(weight[..., None] * acc, axis=0)
    return (numer / denom[..., None]).reshape(numer.shape[0], -1).astype(jnp.bfloat16)


def body(queries, keys, values, block_slots, selected, out_weight):
    ctx_count = lax.axis_size("ctx")
    device = lax.axis_index("ctx")
    head = lax.axis_index("kvh")
    local_blocks = keys.shape[0] // BLKSZ
    last_block = block_slots.shape[0] - 1
    chosen = lax.dynamic_index_in_dim(selected, head, 0, keepdims=False)
    gathered = lax.all_gather(queries, "ctx", axis=0, tiled=True)
    state = (
        jnp.full((QTOK, GROUP), NEG, jnp.float32),
        jnp.zeros((QTOK, GROUP), jnp.float32),
        jnp.zeros((QTOK, GROUP, DH), jnp.float32),
    )
    listed, count, logical = block_pairs(block_slots, chosen, device, local_blocks)
    state = run_list(
        state, listed, 0, count, gathered, keys, values, logical, local_blocks, last_block
    )
    top, total, acc = state
    rows = QTOK // ctx_count
    shaped_top = top.reshape(ctx_count, rows, GROUP)
    shaped_total = total.reshape(ctx_count, rows, GROUP)
    shaped_acc = acc.reshape(ctx_count, rows, GROUP, DH)
    attended = finish(
        (
            lax.all_to_all(shaped_top, "ctx", split_axis=0, concat_axis=0, tiled=True),
            lax.all_to_all(shaped_total, "ctx", split_axis=0, concat_axis=0, tiled=True),
            lax.all_to_all(shaped_acc, "ctx", split_axis=0, concat_axis=0, tiled=True),
        )
    )
    partial_out = jnp.dot(
        lax.all_gather(attended, "ctx", axis=0, tiled=True),
        out_weight,
        preferred_element_type=jnp.float32,
    )
    summed = lax.psum_scatter(partial_out, "kvh", scatter_dimension=0, tiled=True)
    return summed


def solution(mesh):
    return jax.shard_map(
        body,
        mesh=mesh,
        in_specs=(P("ctx", "kvh"), P("ctx", "kvh"), P("ctx", "kvh"), P(), P(), P("kvh", "ctx")),
        out_specs=P("kvh", "ctx"),
        check_vma=False,
    )
```

profile of v0, /device:TPU:6, one launch (start us, length us, event | category | flops | bytes accessed | tf_op | source)
XLA Modules:
  0.0 504.2 jit_solution(2743606866382363788)
XLA Ops:
  6.5 0.7 all-gather.3.cloned.1.call-update
  7.3 0.8 dynamic_slice.56
  8.0 0.7 dynamic-slice_bitcast_fusion
  8.7 0.2 compare_reduce_fusion
  8.9 0.1 reshape.99
  9.0 0.1 reduce-window.8
  9.1 0.1 eq.52
  9.2 0.7 convert_reduce_fusion
  9.8 0.1 add_reduce_fusion
  9.9 0.1 select_reduce_fusion
  10.0 87.8 %all-gather.3.cloned.1.call-done = bf16[512,2048]{1,0:T(8,128)(2,1)} async-done(((bf16[8,2048]{1,0:T(8,128)(2,1)}), bf16[512,2048]{1,0:T(8,128)(2,1)}) %all-gather.3.cloned.1.call-update) | async-done | bytes 2097168 | tf_op jit(solution)/shard_map/all_gather | solution.py:93
  97.9 2.4 broadcast_in_dim.56
  100.3 40.0 %while.16 = (s32[]{:T(128)}, f32[512,16]{0,1:T(8,128)S(1)}, f32[512,16]{0,1:T(8,128)S(1)}, f32[512,16,128]{2,0,1:T(8,128)}, s32[]{:T(128)}, /*index=5*/s32[32]{0...) while((s32[]{:T(128)}, f32[512,16]{0,1:T(8,128)S(1)}, ...), condition=%wide.region_7.8_spmd, body=%wide.region_4.7_spmd.sunk | while | flops 549064832 | bytes 18081372 | solution.py:74
  100.9 0.6 dynamic_slice.87
  104.0 0.6 dynamic_slice.88
  105.2 0.1 fusion.38
  105.4 1.1 constant_dynamic-slice_fusion.2
  106.5 0.3 copy.56
  106.7 1.8 fusion.39
  108.6 1.3 fusion.40
  109.9 3.5 fusion.41
  114.1 0.6 dynamic_slice.87
  117.2 0.6 dynamic_slice.88
  118.4 0.1 fusion.38
  118.5 1.1 constant_dynamic-slice_fusion.2
  119.6 0.3 copy.56
  119.9 1.8 fusion.39
  121.7 1.3 fusion.40
  123.1 3.5 fusion.41
  127.2 0.6 dynamic_slice.87
  130.3 0.6 dynamic_slice.88
  131.5 0.1 fusion.38
  131.6 1.1 constant_dynamic-slice_fusion.2
  132.7 0.3 copy.56
  133.0 1.8 fusion.39
  134.9 1.3 fusion.40
  136.2 3.5 fusion.41
  140.3 0.1 copy.48
  140.5 0.8 reshape.103
  141.2 97.5 %all-to-all-start.2 = ((f32[64,1,128]{2,1,0:T(1,128)}), f32[64,1,128]{2,1,0:T(1,128)S(1)}, u32[]{:S(2)}, u32[]{:S(2)}) async-start(f32[64,1,128]{2,1,0:T(1,128)} %reshape.103), calls=%async_computation.2 | async-start | bytes 65536 | tf_op jit(solution)/shard_map/all_to_all | solution.py:111
  238.7 0.1 copy.43
  238.8 0.8 reshape.101
  239.6 6.9 %all-to-all-done.2 = f32[64,1,128]{2,1,0:T(1,128)S(1)} async-done(((f32[64,1,128]{2,1,0:T(1,128)}), f32[64,1,128]{2,1,0:T(1,128)S(1)}, u32[]{:S(2)}, u32[]{:S(2)}) %all-to-all-start.2) | async-done | bytes 32800 | tf_op jit(solution)/shard_map/all_to_all | solution.py:111
  246.5 6.2 %all-to-all-start = ((f32[64,1,128]{2,1,0:T(1,128)}), f32[64,1,128]{2,1,0:T(1,128)S(1)}, u32[]{:S(2)}, u32[]{:S(2)}) async-start(f32[64,1,128]{2,1,0:T(1,128)} %reshape.101), calls=%async_computation | async-start | bytes 65536 | tf_op jit(solution)/shard_map/all_to_all | solution.py:110
  252.7 4.7 copy.46
  257.3 3.3 all-to-all-done
  260.6 7.3 %all-to-all-start.1 = ((f32[64,8,16,128]{3,1,2,0:T(8,128)}), f32[64,8,16,128]{3,1,2,0:T(8,128)}, u32[]{:S(2)}, u32[]{:S(2)}) async-start(f32[64,8,16,128]{3,1,2,0:T(8,128)} %copy.46), calls=%async_computation.1 | async-start | bytes 8388608 | tf_op jit(solution)/shard_map/all_to_all | solution.py:112
  267.9 0.0 all-gather.5.cloned.1.call-start
  268.0 0.5 broadcast.69
  268.5 0.7 reduce.3
  269.2 0.1 reshape.104
  269.3 0.7 reduce.4
  270.1 0.1 reshape.102
  270.2 0.1 reduce_max.21
  270.3 0.1 multiply_reduce_fusion.1
  270.3 0.2 copy.44
  270.6 0.1 copy.49
  270.6 93.4 %all-to-all-done.1 = f32[64,8,16,128]{3,1,2,0:T(8,128)} async-done(((f32[64,8,16,128]{3,1,2,0:T(8,128)}), f32[64,8,16,128]{3,1,2,0:T(8,128)}, u32[]{:S(2)}, u32[]{:S(2)}) %all-to-all-start.1) | async-done | bytes 4194336 | tf_op jit(solution)/shard_map/all_to_all | solution.py:112
  364.1 2.9 multiply_reduce_fusion
  367.0 0.7 fusion.22
  367.7 0.0 reduce-scatter.2.cloned.1.call-start
  367.7 89.1 %all-gather.5.cloned.1.call-done = bf16[512,2048]{1,0:T(8,128)(2,1)} async-done(((bf16[8,2048]{1,0:T(8,128)(2,1)}), bf16[512,2048]{1,0:T(8,128)(2,1)}) %all-gather.5.cloned.1.call-update) | async-done | bytes 2097168 | tf_op jit(solution)/shard_map/all_gather | solution.py:116
  456.8 3.1 fusion.24
  459.9 37.8 %reduce-scatter.2.cloned.1.call-done = f32[64,256]{1,0:T(8,128)} async-done(((f32[512,256]{1,0:T(8,128)}), f32[64,256]{1,0:T(8,128)}) %reduce-scatter.2.cloned.1.call-update) | async-done | bytes 65552 | tf_op jit(solution)/shard_map/reduce_scatter | solution.py:120
  (23 shorter events, 0.2 us)
Async XLA Ops:
  6.5 450.3 %copy-start = (bf16[2048,256]{1,0:T(8,128)(2,1)S(1)}, bf16[2048,256]{1,0:T(8,128)(2,1)}, u32[]{:S(2)}) copy-start(bf16[2048,256]{1,0:T(8,128)(2,1)} %param.13) | copy-start | bytes 3145732
  6.5 91.3 %all-gather.3.cloned.1.call-start = ((), (), s32[]{:S(2)}) async-start(), calls=%async_computation.4 | async-start | bytes 2129920 | tf_op jit(solution)/shard_map/all_gather | solution.py:93
  141.2 105.3 %all-to-all-start.2 = ((f32[64,1,128]{2,1,0:T(1,128)}), f32[64,1,128]{2,1,0:T(1,128)S(1)}, u32[]{:S(2)}, u32[]{:S(2)}) async-start(f32[64,1,128]{2,1,0:T(1,128)} %reshape.103), calls=%async_computation.2 | async-start | bytes 65536 | tf_op jit(solution)/shard_map/all_to_all | solution.py:111
  246.5 14.1 %all-to-all-start = ((f32[64,1,128]{2,1,0:T(1,128)}), f32[64,1,128]{2,1,0:T(1,128)S(1)}, u32[]{:S(2)}, u32[]{:S(2)}) async-start(f32[64,1,128]{2,1,0:T(1,128)} %reshape.101), calls=%async_computation | async-start | bytes 65536 | tf_op jit(solution)/shard_map/all_to_all | solution.py:110
  260.6 103.5 %all-to-all-start.1 = ((f32[64,8,16,128]{3,1,2,0:T(8,128)}), f32[64,8,16,128]{3,1,2,0:T(8,128)}, u32[]{:S(2)}, u32[]{:S(2)}) async-start(f32[64,8,16,128]{3,1,2,0:T(8,128)} %copy.46), calls=%async_computation.1 | async-start | bytes 8388608 | tf_op jit(solution)/shard_map/all_to_all | solution.py:112
  267.9 188.9 %all-gather.5.cloned.1.call-start = ((), (), s32[]{:S(2)}) async-start(), calls=%async_computation.5 | async-start | bytes 2129920 | tf_op jit(solution)/shard_map/all_gather | solution.py:116
  367.7 130.0 %reduce-scatter.2.cloned.1.call-start = ((), (), s32[]{:S(2)}) async-start(), calls=%async_computation.6 | async-start | bytes 589824 | tf_op jit(solution)/shard_map/reduce_scatter | solution.py:120
Sparse Core Ops, SparseCore 0:
  10.7 87.1 all-gather.2
  367.8 88.9 all-gather.4
  460.0 37.6 reduce-scatter.1
where the time goes:
time: 506 us; the launch traced here: 504 us
  waiting for transfers between devices  319 us (63%)
  starting transfers between devices  111 us (22%)
  local copies, waits for them, and re-layouts  19.3 us (4%)
  matrix products  19 us (4%)
  between operations  13.2 us (3%)
  loops' own time  12 us (2%)
  other arithmetic  10.6 us (2%)
    all_to_all x1, starting transfers between devices, body(): lax.all_to_all(shaped_total, 'ctx', split_axis=0, concat_axis=0, tiled=True)  97.5 us
    all_to_all x1, waiting for transfers between devices, body(): lax.all_to_all(shaped_acc, 'ctx', split_axis=0, concat_axis=0, tiled=True)  93.4 us
    all_gather x1, waiting for transfers between devices, body(): lax.all_gather(attended, 'ctx', axis=0, tiled=True)  89.1 us
    all_gather x1, waiting for transfers between devices, body(): gathered = lax.all_gather(queries, 'ctx', axis=0, tiled=True)  87.8 us
    reduce_scatter x1, waiting for transfers between devices, body(): lax.psum_scatter(partial_out, 'kvh', scatter_dimension=0, tiled=True)  37.8 us
    another operation x1, loops' own time, run_list(): return lax.fori_loop(start, stop, advance, state)  12 us
    dot_general x3, matrix products, attend_pair(): jnp.einsum('rgk,kd->rgd', weights, vblk, preferred_element_type=jnp.float32)  10.4 us
  transfers between devices with their start and end apart: 6, of which 6 were waited for; matrix products, arithmetic and copies ran while one was open for 2% of the time, Pallas kernels for 0%

commit v1 on v0

v1 whole, which is shorter than its diff:
```python
import math

import jax
import jax.numpy as jnp
import numpy as np
from jax import lax
from jax.experimental import pallas as pl
from jax.experimental.pallas import tpu as pltpu
from jax.sharding import PartitionSpec as P

DH = 128
GROUP = 16
BLKSZ = 512
QBLK = 128
NQB = 4
ZN = 8
XN = 4
YN = 8
ROWS = 8
WIDE = GROUP * DH
STATE = WIDE + 128
SCALE = math.log2(math.e) / math.sqrt(DH)
NEG = -(2.0**100)
VMEM_LIMIT = 48 * 1024 * 1024
F32 = jnp.float32
BF16 = jnp.bfloat16


def place(z, x, core):
    return (z * XN + x) * 2 + core


Z_GROUPS = [[place(z, x, c) for z in range(ZN)] for x in range(XN) for c in range(2)]
X_GROUPS = [[place(z, x, c) for x in range(XN)] for z in range(ZN) for c in range(2)]
YC_GROUPS = [
    [place(z, x, c) * YN + y for c in range(2) for y in range(YN)]
    for z in range(ZN)
    for x in range(XN)
]
CORE_SWAP = [(place(z, x, c), place(z, x, 1 - c)) for z in range(ZN) for x in range(XN) for c in range(2)]


def exchange(blocks, axis, groups):
    return lax.all_to_all(
        blocks, axis, split_axis=0, concat_axis=0, tiled=True, axis_index_groups=groups
    )


def spread(rows, axis, groups):
    count = len(groups[0])
    return exchange(jnp.broadcast_to(rows[None], (count,) + rows.shape), axis, groups)


def in_vmem():
    return pl.BlockSpec(memory_space=pltpu.VMEM)


def in_smem():
    return pl.BlockSpec(memory_space=pltpu.SMEM)


def attend_kernel(hits_ref, core_ref, q_ref, k0_ref, v0_ref, k1_ref, v1_ref, out_ref, top, total, acc):
    tile = GROUP * 16
    blocks = k0_ref.shape[0] // BLKSZ
    core = core_ref[0]

    def one_block(c, k_ref, v_ref, b, masked):
        start = pl.multiple_of(b * BLKSZ, BLKSZ)
        kblk = k_ref[pl.ds(start, BLKSZ), :]
        vblk = v_ref[pl.ds(start, BLKSZ), :]
        for x in range(XN):
            qt = jnp.concatenate(
                [q_ref[x, c, :, h * DH : (h + 1) * DH] for h in range(GROUP)], axis=0
            )
            scores = (
                lax.dot_general(qt, kblk, (((1,), (1,)), ((), ())), preferred_element_type=F32)
                * SCALE
            )
            if masked:
                row = lax.broadcasted_iota(jnp.int32, (tile, BLKSZ), 0) % 16
                token = (((2 * c + row // 8) * XN + x) * 2 + core) * ROWS + row % 8
                kpos = lax.broadcasted_iota(jnp.int32, (tile, BLKSZ), 1)
                scores = jnp.where(kpos <= token, scores, NEG)
            old_top = top[x]
            new_top = jnp.maximum(old_top, jnp.max(scores, axis=1, keepdims=True))
            fade = jnp.exp2(old_top - new_top)
            parts = []
            added = None
            for j in range(BLKSZ // 128):
                part = jnp.exp2(scores[:, j * 128 : (j + 1) * 128] - new_top)
                added = part if added is None else added + part
                parts.append(part.astype(BF16))
            probs = jnp.concatenate(parts, axis=1)
            top[x] = new_top
            total[x] = total[x] * fade + added
            acc[x] = acc[x] * fade + jnp.dot(probs, vblk, preferred_element_type=F32)

    def query_block(c, carry):
        top[...] = jnp.full(top.shape, NEG, F32)
        total[...] = jnp.zeros(total.shape, F32)
        acc[...] = jnp.zeros(acc.shape, F32)
        for side, (k_ref, v_ref) in enumerate(((k0_ref, v0_ref), (k1_ref, v1_ref))):

            def step(b, carry, side=side, k_ref=k_ref, v_ref=v_ref):
                kind = hits_ref[c, side * blocks + b]

                @pl.when(kind == 1)
                def _():
                    one_block(c, k_ref, v_ref, b, False)

                @pl.when(kind == 2)
                def _():
                    one_block(c, k_ref, v_ref, b, True)

                return carry

            lax.fori_loop(0, blocks, step, 0)
        first = pl.multiple_of(c * 16, 16)
        lane = lax.broadcasted_iota(jnp.int32, (16, 128), 1)
        for x in range(XN):
            peak = top[x]
            kept = peak.astype(BF16).astype(F32)
            factor = jnp.exp2(peak - kept)
            scaled = (acc[x] * factor).astype(BF16)
            summed = jnp.sum(total[x], axis=1, keepdims=True) * factor
            high = summed.astype(BF16).astype(F32)
            low = summed - high
            stats = jnp.zeros((16, 128), F32)
            for h in range(GROUP):
                rows = slice(h * 16, (h + 1) * 16)
                out_ref[x, pl.ds(first, 16), h * DH : (h + 1) * DH] = scaled[rows]
                stats = jnp.where(lane == h, kept[rows], stats)
                stats = jnp.where(lane == GROUP + h, high[rows], stats)
                stats = jnp.where(lane == 2 * GROUP + h, low[rows], stats)
            out_ref[x, pl.ds(first, 16), WIDE:] = stats.astype(BF16)
        return carry

    lax.fori_loop(0, NQB, query_block, 0)


def attend(hits, core, q, k0, v0, k1, v1):
    tile = GROUP * 16
    return pl.pallas_call(
        attend_kernel,
        out_shape=jax.ShapeDtypeStruct((XN, NQB * 16, STATE), BF16),
        in_specs=[in_smem(), in_smem()] + [in_vmem()] * 5,
        out_specs=in_vmem(),
        scratch_shapes=[
            pltpu.VMEM((XN, tile, 128), F32),
            pltpu.VMEM((XN, tile, 128), F32),
            pltpu.VMEM((XN, tile, DH), F32),
        ],
        compiler_params=pltpu.CompilerParams(vmem_limit_bytes=VMEM_LIMIT),
    )(hits, core, q, k0, v0, k1, v1)


def weights_of(stats):
    tops = [s[:, :GROUP] for s in stats]
    peak = tops[0]
    for t in tops[1:]:
        peak = jnp.maximum(peak, t)
    weights = [jnp.exp2(t - peak) for t in tops]
    total = None
    for w, s in zip(weights, stats):
        term = w * (s[:, GROUP : 2 * GROUP] + s[:, 2 * GROUP : 3 * GROUP])
        total = term if total is None else total + term
    return peak, weights, total


def merge_kernel(in_ref, out_ref):
    count, rows = in_ref.shape[0], in_ref.shape[1]
    for r in range(0, rows, 16):
        stats = [in_ref[s, r : r + 16, WIDE:].astype(F32) for s in range(count)]
        peak, weights, total = weights_of(stats)
        for h in range(GROUP):
            cols = slice(h * DH, (h + 1) * DH)
            value = None
            for s in range(count):
                term = in_ref[s, r : r + 16, cols].astype(F32) * weights[s][:, h : h + 1]
                value = term if value is None else value + term
            out_ref[r : r + 16, cols] = value.astype(BF16)
        high = total.astype(BF16).astype(F32)
        rest = jnp.zeros((16, 128 - 3 * GROUP), F32)
        out_ref[r : r + 16, WIDE:] = jnp.concatenate([peak, high, total - high, rest], axis=1).astype(BF16)


def merge(states):
    return pl.pallas_call(
        merge_kernel,
        out_shape=jax.ShapeDtypeStruct(states.shape[1:], BF16),
        in_specs=[in_vmem()],
        out_specs=in_vmem(),
        compiler_params=pltpu.CompilerParams(vmem_limit_bytes=VMEM_LIMIT),
    )(states)


def finish_kernel(in_ref, out_ref):
    pairs = in_ref.shape[0] // 16
    stats = []
    for i in range(pairs):
        both = in_ref[i * 16 : (i + 1) * 16, WIDE:].astype(F32)
        stats += [both[:ROWS], both[ROWS:]]
    _, weights, total = weights_of(stats)
    inverse = 1.0 / total
    weights = [w * inverse for w in weights]
    for h in range(GROUP):
        cols = slice(h * DH, (h + 1) * DH)
        value = None
        for i in range(pairs):
            both = in_ref[i * 16 : (i + 1) * 16, cols].astype(F32)
            term = (
                both[:ROWS] * weights[2 * i][:, h : h + 1]
                + both[ROWS:] * weights[2 * i + 1][:, h : h + 1]
            )
            value = term if value is None else value + term
        twice = jnp.concatenate([value, value], axis=0).astype(BF16)
        for i in range(pairs):
            out_ref[i * 16 : (i + 1) * 16, cols] = twice


def finish(states):
    return pl.pallas_call(
        finish_kernel,
        out_shape=jax.ShapeDtypeStruct((ZN * ROWS, WIDE), BF16),
        in_specs=[in_vmem()],
        out_specs=in_vmem(),
        compiler_params=pltpu.CompilerParams(vmem_limit_bytes=VMEM_LIMIT),
    )(states)


def project_kernel(core_ref, a_ref, w0_ref, w1_ref, out_ref):
    core = core_ref[0]
    rows = a_ref[...].reshape(XN * ZN * ROWS, WIDE)
    for side, w_ref in enumerate((w0_ref, w1_ref)):
        result = jnp.dot(rows, w_ref[...], preferred_element_type=F32)
        target = core if side == 0 else 1 - core
        for z in range(ZN):
            chunk = jnp.concatenate(
                [result[(x * ZN + z) * ROWS : (x * ZN + z + 1) * ROWS] for x in range(XN)], axis=0
            )
            out_ref[target, z] = chunk.astype(BF16)


def project(core, rows, w0, w1):
    return pl.pallas_call(
        project_kernel,
        out_shape=jax.ShapeDtypeStruct((2, ZN, XN * ROWS, w0.shape[1]), BF16),
        in_specs=[in_smem()] + [in_vmem()] * 3,
        out_specs=in_vmem(),
        compiler_params=pltpu.CompilerParams(vmem_limit_bytes=VMEM_LIMIT),
    )(core, rows, w0, w1)


def find_hits(block_slots, selected, device, head, local_blocks):
    chosen = lax.dynamic_index_in_dim(selected, head, 0, keepdims=False)
    pair = lax.dynamic_slice_in_dim(block_slots, device // 2 * 2 * local_blocks, 2 * local_blocks)
    pair = pair.reshape(2, local_blocks)
    logical = jnp.where(device % 2 == 0, pair, pair[::-1]).reshape(-1)
    hit = jnp.any(chosen[:, None, :] == logical[None, :, None], axis=2).astype(jnp.int32)
    last = (logical == block_slots.shape[0] - 1).astype(jnp.int32)
    return hit * (1 + last[None, :])


def body(queries, keys, values, block_slots, selected, out_weight):
    device = lax.axis_index("ctx")
    head = lax.axis_index("kvh")
    core = (device % 2).reshape(1).astype(jnp.int32)
    hits = find_hits(block_slots, selected, device, head, keys.shape[0] // BLKSZ)
    other_keys = lax.ppermute(keys, "ctx", CORE_SWAP)
    other_values = lax.ppermute(values, "ctx", CORE_SWAP)
    other_weight = lax.ppermute(out_weight, "ctx", CORE_SWAP)

    column = spread(queries, "ctx", Z_GROUPS).reshape(ZN * ROWS, WIDE)
    plane = spread(column, "ctx", X_GROUPS).reshape(XN, NQB, 16, WIDE)
    states = attend(hits, core, plane, keys, values, other_keys, other_values)
    merged = merge(exchange(states, "ctx", X_GROUPS))
    arrived = exchange(merged.reshape(ZN, ROWS, STATE), "ctx", Z_GROUPS)
    attended = finish(arrived.reshape(ZN * ROWS, STATE)).reshape(ZN, ROWS, WIDE)

    column = exchange(attended, "ctx", Z_GROUPS).reshape(ZN * ROWS, WIDE)
    plane = spread(column, "ctx", X_GROUPS)
    shares = project(core, plane, out_weight, other_weight)
    arrived = exchange(shares.reshape(2 * YN, XN * ROWS, -1), ("ctx", "kvh"), YC_GROUPS)
    summed = jnp.sum(arrived.reshape(2, YN, XN, ROWS, -1).astype(F32), axis=1)
    return jnp.swapaxes(summed, 0, 1).reshape(XN * 2 * ROWS, -1)


def solution(mesh):
    return jax.shard_map(
        body,
        mesh=mesh,
        in_specs=(P("ctx", "kvh"), P("ctx", "kvh"), P("ctx", "kvh"), P(), P(), P("kvh", "ctx")),
        out_specs=P("kvh", "ctx"),
        check_vma=False,
    )
```

time: 506 us -> 150 us (0.30)
  the two profiles are of different devices: /device:TPU:6 before, /device:TPU:8 now
where the time goes in v1:
time: 150 us; the launch traced here: 149 us
  blocking collectives  59.3 us (40%)
  waiting for transfers between devices  38.9 us (26%)
  starting transfers between devices  27.9 us (19%)
  Pallas kernels  17.3 us (12%)
  local copies, waits for them, and re-layouts  5.27 us (4%)
    all_to_all x3, blocking collectives, exchange(): lax.all_to_all(blocks, axis, split_axis=0, concat_axis=0, tiled=True, axi...  59.3 us
    all_to_all x4, waiting for transfers between devices, exchange(): lax.all_to_all(blocks, axis, split_axis=0, concat_axis=0, tiled=True, axi...  38.9 us
    all_to_all x4, starting transfers between devices, exchange(): lax.all_to_all(blocks, axis, split_axis=0, concat_axis=0, tiled=True, axi...  21.7 us
    pallas_call x1, Pallas kernels, attend(): pl.pallas_call(attend_kernel, out_shape=jax.ShapeDtypeStruct((XN, NQB * 1...  13.8 us
    broadcast_in_dim x3, local copies, waits for them, and re-layouts, spread(): jnp.broadcast_to(rows[None], (count,) + rows.shape)  3.65 us
  transfers between devices with their start and end apart: 7, of which 4 were waited for; matrix products, arithmetic and copies ran while one was open for 2% of the time, Pallas kernels for 0%

profile of v1, /device:TPU:8, one launch (start us, length us, event | category | flops | bytes accessed | tf_op | source)
XLA Modules:
  0.0 149.1 jit_solution(16010287923675763129)
XLA Ops:
  0.0 0.0 copy-start
  0.0 1.5 broadcast_in_dim.10
  1.5 10.3 %all-to-all-start = ((bf16[8,8,2048]{2,1,0:T(8,128)(2,1)}), bf16[8,8,2048]{2,1,0:T(8,128)(2,1)S(1)}, u32[]{:S(2)}, u32[]{:S(2)}) async-start(bf16[8,8,2048]{2,1,0:T(8,128)(2,1)} %broadcast_in_dim.10), calls=%async_computation | async-start | bytes 524288 | tf_op jit(solution)/shard_map/all_to_all | solution.py:44
  11.8 1.9 %collective-permute-start = (bf16[4096,128]{1,0:T(8,128)(2,1)}, bf16[4096,128]{1,0:T(8,128)(2,1)}, u32[]{:S(2)}, u32[]{:S(2)}) collective-permute-start(bf16[4096,128]{1,0:T(8,128)(2,1)} %k0_ref.1), channel_id=1, source_target_pairs={{0,8},{8,0},{16,24},{24,16},{32,40},{40,32},{48,56},{56,48},{64,72... | collective-permute-start | bytes 3145736 | tf_op jit(solution)/shard_map/ppermute | solution.py:269
  13.7 2.4 %collective-permute-start.1 = (bf16[4096,128]{1,0:T(8,128)(2,1)}, bf16[4096,128]{1,0:T(8,128)(2,1)}, u32[]{:S(2)}, u32[]{:S(2)}) collective-permute-start(bf16[4096,128]{1,0:T(8,128)(2,1)} %v0_ref.1), channel_id=1, source_target_pairs={{0,8},{8,0},{16,24},{24,16},{32,40},{40,32},{48,56},{56,48},{64,72... | collective-permute-start | bytes 3145736 | tf_op jit(solution)/shard_map/ppermute | solution.py:270
  16.2 0.8 dynamic_slice.8
  16.9 0.1 reshape.43
  17.0 6.6 %all-to-all-done = bf16[8,8,2048]{2,1,0:T(8,128)(2,1)S(1)} async-done(((bf16[8,8,2048]{2,1,0:T(8,128)(2,1)}), bf16[8,8,2048]{2,1,0:T(8,128)(2,1)S(1)}, u32[]{:S(2)}, u32[]{:S(2)}) %all-to-all-start) | async-done | bytes 262176 | tf_op jit(solution)/shard_map/all_to_all | solution.py:44
  23.7 1.1 broadcast_in_dim.24
  24.8 0.0 copy-start.2
  24.8 0.0 copy-start.3
  24.8 4.4 %all-to-all-start.1 = ((bf16[4,64,2048]{2,1,0:T(8,128)(2,1)}), bf16[4,64,2048]{2,1,0:T(8,128)(2,1)S(1)}, u32[]{:S(2)}, u32[]{:S(2)}) async-start(bf16[4,64,2048]{2,1,0:T(8,128)(2,1)} %broadcast_in_dim.24), calls=%async_computation.1 | async-start | bytes 2097152 | tf_op jit(solution)/shard_map/all_to_all | solution.py:44
  29.2 0.1 eq.33
  29.3 0.0 copy-done
  29.3 0.2 compare_reduce_fusion
  29.5 0.0 collective-permute-done.k1_ref
  29.5 0.0 collective-permute-done.1.v1_ref
  29.5 13.0 %all-to-all-done.1 = bf16[4,64,2048]{2,1,0:T(8,128)(2,1)S(1)} async-done(((bf16[4,64,2048]{2,1,0:T(8,128)(2,1)}), bf16[4,64,2048]{2,1,0:T(8,128)(2,1)S(1)}, u32[]{:S(2)}, u32[]{:S(2)}) %all-to-all-start.1) | async-done | bytes 1048608 | tf_op jit(solution)/shard_map/all_to_all | solution.py:44
  42.5 0.0 copy-done.2
  42.5 0.0 copy-done.3
  42.5 13.8 %shard_map.64 = bf16[4,64,2176]{2,1,0:T(8,128)(2,1)} custom-call(s32[4,16]{1,0:T(4,128)S(1)} %broadcast_select_fusion.hits_ref, s32[1]{0:T(128)} %bitcast.core_ref, bf16[4,4,16,2048]{3,2,1,0:T(8,128)(2,1)S(1)} %bitcast.14, bf16[4096,128]{1,0:T(8,128)(2,1)S(1)} %copy-done.2, bf16[4096,128]{1,0:T(8,128)(2,1)S(1)} %copy-done.3, ...), custom_call_target="tpu_custom_call" | custom-call | tf_op jit(solution)/shard_map/pallas_call | solution.py:143
  56.3 24.4 %all_to_all.35.in_ref = bf16[4,64,2176]{2,1,0:T(8,128)(2,1)S(1)} all-to-all(bf16[4,64,2176]{2,1,0:T(8,128)(2,1)} %shard_map.64), channel_id=1, replica_groups={{0,16,32,48},{8,24,40,56},{64,80,96,112},{72,88,104,120},{128,144,160,1..., dimensions={0} | all-to-all | bytes 2228224 | tf_op jit(solution)/shard_map/all_to_all | solution.py:44
  80.8 1.7 %shard_map.65 = bf16[64,2176]{1,0:T(8,128)(2,1)S(1)} custom-call(bf16[4,64,2176]{2,1,0:T(8,128)(2,1)S(1)} %all_to_all.35.in_ref), custom_call_target="tpu_custom_call" | custom-call | tf_op jit(solution)/shard_map/pallas_call | solution.py:188
  82.5 0.0 copy-start.1
  82.5 20.8 %all_to_all.36 = bf16[8,8,2176]{2,1,0:T(8,128)(2,1)S(1)} all-to-all(bf16[8,8,2176]{2,1,0:T(8,128)(2,1)S(1)} %bitcast.15), channel_id=1, replica_groups={{0,64,128,192,256,320,384,448},{8,72,136,200,264,328,392,456},{16,80,14..., dimensions={0} | all-to-all | bytes 557056 | tf_op jit(solution)/shard_map/all_to_all | solution.py:44
  103.3 1.1 shard_map.66
  104.4 3.4 %all-to-all-start.4 = ((bf16[8,8,2048]{2,1,0:T(8,128)(2,1)}), bf16[8,8,2048]{2,1,0:T(8,128)(2,1)S(1)}, u32[]{:S(2)}, u32[]{:S(2)}) async-start(bf16[8,8,2048]{2,1,0:T(8,128)(2,1)} %bitcast.6), calls=%async_computation.4 | async-start | bytes 524288 | tf_op jit(solution)/shard_map/all_to_all | solution.py:44
  107.8 0.0 copy-done.1
  107.8 1.9 %collective-permute-start.2 = (bf16[2048,256]{1,0:T(8,128)(2,1)S(1)}, bf16[2048,256]{1,0:T(8,128)(2,1)S(1)}, u32[]{:S(2)}, u32[]{:S(2)}) collective-permute-start(bf16[2048,256]{1,0:T(8,128)(2,1)S(1)} %copy-done.1), channel_id=1, source_target_pairs={{0,8},{8,0},{16,24},{24,16},{32,40},{40,32},{48,56},{56,48},{64,72... | collective-permute-start | bytes 3145736 | tf_op jit(solution)/shard_map/ppermute | solution.py:271
  109.7 8.5 %all-to-all-done.4 = bf16[8,8,2048]{2,1,0:T(8,128)(2,1)S(1)} async-done(((bf16[8,8,2048]{2,1,0:T(8,128)(2,1)}), bf16[8,8,2048]{2,1,0:T(8,128)(2,1)S(1)}, u32[]{:S(2)}, u32[]{:S(2)}) %all-to-all-start.4) | async-done | bytes 262176 | tf_op jit(solution)/shard_map/all_to_all | solution.py:44
  118.2 1.1 broadcast_in_dim.26
  119.3 3.5 %all-to-all-start.5 = ((bf16[4,64,2048]{2,1,0:T(8,128)(2,1)}), bf16[4,64,2048]{2,1,0:T(8,128)(2,1)S(1)}, u32[]{:S(2)}, u32[]{:S(2)}) async-start(bf16[4,64,2048]{2,1,0:T(8,128)(2,1)} %broadcast_in_dim.26), calls=%async_computation.5 | async-start | bytes 2097152 | tf_op jit(solution)/shard_map/all_to_all | solution.py:44
  122.8 0.0 collective-permute-done.2.w1_ref
  122.8 10.8 %all-to-all-done.5.a_ref = bf16[4,64,2048]{2,1,0:T(8,128)(2,1)S(1)} async-done(((bf16[4,64,2048]{2,1,0:T(8,128)(2,1)}), bf16[4,64,2048]{2,1,0:T(8,128)(2,1)S(1)}, u32[]{:S(2)}, u32[]{:S(2)}) %all-to-all-start.5) | async-done | bytes 1048608 | tf_op jit(solution)/shard_map/all_to_all | solution.py:44
  133.7 0.7 shard_map.67
  134.4 14.0 %all_to_all.37 = bf16[16,32,256]{2,1,0:T(8,128)(2,1)S(1)} all-to-all(bf16[16,32,256]{2,1,0:T(8,128)(2,1)S(1)} %bitcast.17), channel_id=1, replica_groups={{0,1,2,3,4,5,6,7,8,9,10,11,12,13,14,15},{16,17,18,19,20,21,22,23,24,25,..., dimensions={0} | all-to-all | bytes 524288 | tf_op jit(solution)/shard_map/all_to_all | solution.py:44
  148.5 0.6 copy.8
  (6 shorter events, 0.1 us)
Async XLA Ops:
  0.0 29.3 %copy-start = (s32[8,4,64]{2,1,0:T(4,128)S(1)}, s32[8,4,64]{2,1,0:T(4,128)}, u32[]{:S(2)}) copy-start(s32[8,4,64]{2,1,0:T(4,128)} %param.10) | copy-start | bytes 24580
  1.5 22.2 %all-to-all-start = ((bf16[8,8,2048]{2,1,0:T(8,128)(2,1)}), bf16[8,8,2048]{2,1,0:T(8,128)(2,1)S(1)}, u32[]{:S(2)}, u32[]{:S(2)}) async-start(bf16[8,8,2048]{2,1,0:T(8,128)(2,1)} %broadcast_in_dim.10), calls=%async_computation | async-start | bytes 524288 | tf_op jit(solution)/shard_map/all_to_all | solution.py:44
  11.8 17.7 %collective-permute-start = (bf16[4096,128]{1,0:T(8,128)(2,1)}, bf16[4096,128]{1,0:T(8,128)(2,1)}, u32[]{:S(2)}, u32[]{:S(2)}) collective-permute-start(bf16[4096,128]{1,0:T(8,128)(2,1)} %k0_ref.1), channel_id=1, source_target_pairs={{0,8},{8,0},{16,24},{24,16},{32,40},{40,32},{48,56},{56,48},{64,72... | collective-permute-start | bytes 3145736 | tf_op jit(solution)/shard_map/ppermute | solution.py:269
  13.7 15.8 %collective-permute-start.1 = (bf16[4096,128]{1,0:T(8,128)(2,1)}, bf16[4096,128]{1,0:T(8,128)(2,1)}, u32[]{:S(2)}, u32[]{:S(2)}) collective-permute-start(bf16[4096,128]{1,0:T(8,128)(2,1)} %v0_ref.1), channel_id=1, source_target_pairs={{0,8},{8,0},{16,24},{24,16},{32,40},{40,32},{48,56},{56,48},{64,72... | collective-permute-start | bytes 3145736 | tf_op jit(solution)/shard_map/ppermute | solution.py:270
  24.8 17.7 %copy-start.2 = (bf16[4096,128]{1,0:T(8,128)(2,1)S(1)}, bf16[4096,128]{1,0:T(8,128)(2,1)}, u32[]{:S(2)}) copy-start(bf16[4096,128]{1,0:T(8,128)(2,1)} %k0_ref.1) | copy-start | bytes 3145732
  24.8 17.7 %copy-start.3 = (bf16[4096,128]{1,0:T(8,128)(2,1)S(1)}, bf16[4096,128]{1,0:T(8,128)(2,1)}, u32[]{:S(2)}) copy-start(bf16[4096,128]{1,0:T(8,128)(2,1)} %v0_ref.1) | copy-start | bytes 3145732
  24.8 17.7 %all-to-all-start.1 = ((bf16[4,64,2048]{2,1,0:T(8,128)(2,1)}), bf16[4,64,2048]{2,1,0:T(8,128)(2,1)S(1)}, u32[]{:S(2)}, u32[]{:S(2)}) async-start(bf16[4,64,2048]{2,1,0:T(8,128)(2,1)} %broadcast_in_dim.24), calls=%async_computation.1 | async-start | bytes 2097152 | tf_op jit(solution)/shard_map/all_to_all | solution.py:44
  82.5 25.3 %copy-start.1 = (bf16[2048,256]{1,0:T(8,128)(2,1)S(1)}, bf16[2048,256]{1,0:T(8,128)(2,1)}, u32[]{:S(2)}) copy-start(bf16[2048,256]{1,0:T(8,128)(2,1)} %w0_ref.1) | copy-start | bytes 3145732
  104.4 13.8 %all-to-all-start.4 = ((bf16[8,8,2048]{2,1,0:T(8,128)(2,1)}), bf16[8,8,2048]{2,1,0:T(8,128)(2,1)S(1)}, u32[]{:S(2)}, u32[]{:S(2)}) async-start(bf16[8,8,2048]{2,1,0:T(8,128)(2,1)} %bitcast.6), calls=%async_computation.4 | async-start | bytes 524288 | tf_op jit(solution)/shard_map/all_to_all | solution.py:44
  107.8 15.0 %collective-permute-start.2 = (bf16[2048,256]{1,0:T(8,128)(2,1)S(1)}, bf16[2048,256]{1,0:T(8,128)(2,1)S(1)}, u32[]{:S(2)}, u32[]{:S(2)}) collective-permute-start(bf16[2048,256]{1,0:T(8,128)(2,1)S(1)} %copy-done.1), channel_id=1, source_target_pairs={{0,8},{8,0},{16,24},{24,16},{32,40},{40,32},{48,56},{56,48},{64,72... | collective-permute-start | bytes 3145736 | tf_op jit(solution)/shard_map/ppermute | solution.py:271
  119.3 14.4 %all-to-all-start.5 = ((bf16[4,64,2048]{2,1,0:T(8,128)(2,1)}), bf16[4,64,2048]{2,1,0:T(8,128)(2,1)S(1)}, u32[]{:S(2)}, u32[]{:S(2)}) async-start(bf16[4,64,2048]{2,1,0:T(8,128)(2,1)} %broadcast_in_dim.26), calls=%async_computation.5 | async-start | bytes 2097152 | tf_op jit(solution)/shard_map/all_to_all | solution.py:44

commit v2 on v1

--- a/solution.py
+++ b/solution.py
@@ -1,8 +1,8 @@
+import functools
 import math
 
 import jax
 import jax.numpy as jnp
-import numpy as np
 from jax import lax
 from jax.experimental import pallas as pl
 from jax.experimental.pallas import tpu as pltpu
@@ -59,99 +59,184 @@
     return pl.BlockSpec(memory_space=pltpu.SMEM)
 
 
-def attend_kernel(hits_ref, core_ref, q_ref, k0_ref, v0_ref, k1_ref, v1_ref, out_ref, top, total, acc):
+def attend_kernel(
+    alone,
+    hits_ref,
+    place_ref,
+    q_ref,
+    k0_ref,
+    v0_ref,
+    k1_ref,
+    v1_ref,
+    *rest,
+):
+    own_ref = None if alone else rest[0]
+    out_ref, top, total, acc, scaled, k_all, v_all, listed, sems = rest[0 if alone else 1 :]
     tile = GROUP * 16
-    blocks = k0_ref.shape[0] // BLKSZ
-    core = core_ref[0]
-
-    def one_block(c, k_ref, v_ref, b, masked):
-        start = pl.multiple_of(b * BLKSZ, BLKSZ)
-        kblk = k_ref[pl.ds(start, BLKSZ), :]
-        vblk = v_ref[pl.ds(start, BLKSZ), :]
-        for x in range(XN):
-            qt = jnp.concatenate(
-                [q_ref[x, c, :, h * DH : (h + 1) * DH] for h in range(GROUP)], axis=0
-            )
-            scores = (
-                lax.dot_general(qt, kblk, (((1,), (1,)), ((), ())), preferred_element_type=F32)
-                * SCALE
-            )
-            if masked:
-                row = lax.broadcasted_iota(jnp.int32, (tile, BLKSZ), 0) % 16
-                token = (((2 * c + row // 8) * XN + x) * 2 + core) * ROWS + row % 8
-                kpos = lax.broadcasted_iota(jnp.int32, (tile, BLKSZ), 1)
-                scores = jnp.where(kpos <= token, scores, NEG)
-            old_top = top[x]
-            new_top = jnp.maximum(old_top, jnp.max(scores, axis=1, keepdims=True))
-            fade = jnp.exp2(old_top - new_top)
-            parts = []
-            added = None
-            for j in range(BLKSZ // 128):
-                part = jnp.exp2(scores[:, j * 128 : (j + 1) * 128] - new_top)
-                added = part if added is None else added + part
-                parts.append(part.astype(BF16))
-            probs = jnp.concatenate(parts, axis=1)
-            top[x] = new_top
-            total[x] = total[x] * fade + added
-            acc[x] = acc[x] * fade + jnp.dot(probs, vblk, preferred_element_type=F32)
+    local = k0_ref.shape[0]
+    blocks = 2 * local // BLKSZ
+    column = place_ref[0]
+    core = place_ref[1]
+    parts = [column] if alone else [lax.rem(column + j, XN) for j in range(1, XN)]
+    copies = []
+    for i, (source, target, start) in enumerate(
+        ((k0_ref, k_all, 0), (v0_ref, v_all, 0), (k1_ref, k_all, local), (v1_ref, v_all, local))
+    ):
+        copy = pltpu.make_async_copy(source, target.at[pl.ds(start, local)], sems.at[i])
+        copy.start()
+        copies.append(copy)
+    if not alone:
+        out_ref[column] = own_ref[...]
+    for copy in copies:
+        copy.wait()
+
+    def block_of(ref, b):
+        return ref[pl.ds(pl.multiple_of(b * BLKSZ, BLKSZ), BLKSZ), :]
+
+    def rows_of(i):
+        return slice(i * tile, (i + 1) * tile)
+
+    def score(i, group):
+        kblk = jnp.concatenate([block_of(k_all, b) for b in group], axis=0)
+        return lax.dot_general(
+            scaled[rows_of(i)],
+            jnp.concatenate([kblk, kblk], axis=1),
+            (((1,), (1,)), ((), ())),
+            preferred_element_type=F32,
+        )
+
+    def soften(i, scores):
+        old_top = top[rows_of(i)]
+        new_top = jnp.maximum(old_top, jnp.max(scores, axis=1, keepdims=True))
+        fade = jnp.exp2(old_top - new_top)
+        probs = []
+        added = None
+        for j in range(scores.shape[1] // 128):
+            part = jnp.exp2(scores[:, j * 128 : (j + 1) * 128] - new_top)
+            added = part if added is None else added + part
+            probs.append(part.astype(BF16))
+        top[rows_of(i)] = new_top
+        total[rows_of(i)] = total[rows_of(i)] * fade + added
+        return jnp.concatenate(probs, axis=1), fade
+
+    def gather(i, group, probs, fade):
+        vblk = jnp.concatenate([block_of(v_all, b) for b in group], axis=0)
+        acc[rows_of(i)] = acc[rows_of(i)] * fade + jnp.dot(probs, vblk, preferred_element_type=F32)
+
+    def run(work, mask=None):
+        scores = score(*work[0])
+        before = None
+        for at, (i, group) in enumerate(work):
+            following = score(*work[at + 1]) if at + 1 < len(work) else None
+            if mask is not None:
+                scores = jnp.where(mask(i), scores, NEG)
+            probs, fade = soften(i, scores)
+            if before is not None:
+                gather(*before)
+            before = (i, group, probs, fade)
+            scores = following
+        gather(*before)
 
     def query_block(c, carry):
         top[...] = jnp.full(top.shape, NEG, F32)
         total[...] = jnp.zeros(total.shape, F32)
         acc[...] = jnp.zeros(acc.shape, F32)
-        for side, (k_ref, v_ref) in enumerate(((k0_ref, v0_ref), (k1_ref, v1_ref))):
-
-            def step(b, carry, side=side, k_ref=k_ref, v_ref=v_ref):
-                kind = hits_ref[c, side * blocks + b]
-
-                @pl.when(kind == 1)
-                def _():
-                    one_block(c, k_ref, v_ref, b, False)
-
-                @pl.when(kind == 2)
-                def _():
-                    one_block(c, k_ref, v_ref, b, True)
-
-                return carry
-
-            lax.fori_loop(0, blocks, step, 0)
+        for i, x in enumerate(parts):
+            source = q_ref.at[c] if alone else q_ref.at[x, c]
+            rows = jnp.concatenate([source[:, h * DH : (h + 1) * DH] for h in range(GROUP)], axis=0)
+            rows = rows.astype(F32) * SCALE
+            high = rows.astype(BF16)
+            low = (rows - high.astype(F32)).astype(BF16)
+            scaled[rows_of(i)] = jnp.concatenate([high, low], axis=1)
+
+        def collect(b, found):
+            listed[found] = b
+            return found + jnp.where(hits_ref[c, b] == 1, 1, 0)
+
+        found = lax.fori_loop(0, blocks, collect, 0)
+        span = range(len(parts))
+
+        def two(j, carry):
+            first, second = listed[2 * j], listed[2 * j + 1]
+            if alone:
+                run([(i, [b]) for b in (first, second) for i in span])
+            else:
+                run([(i, [first, second]) for i in span])
+            return carry
+
+        lax.fori_loop(0, found // 2, two, 0)
+
+        @pl.when(found % 2 == 1)
+        def _():
+            run([(i, [listed[found - 1]]) for i in span])
+
+        def current(b, carry):
+            @pl.when(hits_ref[c, b] == 2)
+            def _():
+                def mask(i):
+                    row = lax.broadcasted_iota(jnp.int32, (tile, BLKSZ), 0) % 16
+                    token = (((2 * c + row // 8) * XN + parts[i]) * 2 + core) * ROWS + row % 8
+                    return lax.broadcasted_iota(jnp.int32, (tile, BLKSZ), 1) <= token
+
+                run([(i, [b]) for i in span], mask)
+
+            return carry
+
+        lax.fori_loop(0, blocks, current, 0)
+
         first = pl.multiple_of(c * 16, 16)
         lane = lax.broadcasted_iota(jnp.int32, (16, 128), 1)
-        for x in range(XN):
-            peak = top[x]
+        for i, x in enumerate(parts):
+            target = out_ref if alone else out_ref.at[x]
+            peak = top[rows_of(i)]
             kept = peak.astype(BF16).astype(F32)
             factor = jnp.exp2(peak - kept)
-            scaled = (acc[x] * factor).astype(BF16)
-            summed = jnp.sum(total[x], axis=1, keepdims=True) * factor
+            values = (acc[rows_of(i)] * factor).astype(BF16)
+            summed = jnp.sum(total[rows_of(i)], axis=1, keepdims=True) * factor
             high = summed.astype(BF16).astype(F32)
             low = summed - high
             stats = jnp.zeros((16, 128), F32)
             for h in range(GROUP):
                 rows = slice(h * 16, (h + 1) * 16)
-                out_ref[x, pl.ds(first, 16), h * DH : (h + 1) * DH] = scaled[rows]
+                target[pl.ds(first, 16), h * DH : (h + 1) * DH] = values[rows]
                 stats = jnp.where(lane == h, kept[rows], stats)
                 stats = jnp.where(lane == GROUP + h, high[rows], stats)
                 stats = jnp.where(lane == 2 * GROUP + h, low[rows], stats)
-            out_ref[x, pl.ds(first, 16), WIDE:] = stats.astype(BF16)
+            target[pl.ds(first, 16), WIDE:] = stats.astype(BF16)
         return carry
 
     lax.fori_loop(0, NQB, query_block, 0)
 
 
-def attend(hits, core, q, k0, v0, k1, v1):
+def attend(alone, hits, where, q, k0, v0, k1, v1, own=None):
+    parts = 1 if alone else XN - 1
     tile = GROUP * 16
+    shape = (NQB * 16, STATE) if alone else (XN, NQB * 16, STATE)
+    operands = (hits, where, q, k0, v0, k1, v1) + (() if alone else (own,))
+    specs = [in_smem(), in_smem(), in_vmem()] + [pl.BlockSpec(memory_space=pl.ANY)] * 4
+    specs += [] if alone else [in_vmem()]
+    pairs = 8 * parts * tile * BLKSZ
     return pl.pallas_call(
-        attend_kernel,
-        out_shape=jax.ShapeDtypeStruct((XN, NQB * 16, STATE), BF16),
-        in_specs=[in_smem(), in_smem()] + [in_vmem()] * 5,
+        functools.partial(attend_kernel, alone),
+        name="attend_own" if alone else "attend_rest",
+        out_shape=jax.ShapeDtypeStruct(shape, BF16),
+        in_specs=specs,
         out_specs=in_vmem(),
         scratch_shapes=[
-            pltpu.VMEM((XN, tile, 128), F32),
-            pltpu.VMEM((XN, tile, 128), F32),
-            pltpu.VMEM((XN, tile, DH), F32),
+            pltpu.VMEM((parts * tile, 128), F32),
+            pltpu.VMEM((parts * tile, 128), F32),
+            pltpu.VMEM((parts * tile, DH), F32),
+            pltpu.VMEM((parts * tile, 2 * DH), BF16),
+            pltpu.VMEM((2 * k0.shape[0], DH), BF16),
+            pltpu.VMEM((2 * k0.shape[0], DH), BF16),
+            pltpu.SMEM((2 * k0.shape[0] // BLKSZ + 8,), jnp.int32),
+            pltpu.SemaphoreType.DMA((4,)),
         ],
         compiler_params=pltpu.CompilerParams(vmem_limit_bytes=VMEM_LIMIT),
-    )(hits, core, q, k0, v0, k1, v1)
+        cost_estimate=pl.CostEstimate(
+            flops=pairs * 4 * DH, bytes_accessed=8 * 1024 * 1024, transcendentals=pairs
+        ),
+    )(*operands)
 
 
 def weights_of(stats):
@@ -265,14 +350,17 @@
     device = lax.axis_index("ctx")
     head = lax.axis_index("kvh")
     core = (device % 2).reshape(1).astype(jnp.int32)
+    where = jnp.stack([device // 2 % XN, device % 2]).astype(jnp.int32)
     hits = find_hits(block_slots, selected, device, head, keys.shape[0] // BLKSZ)
     other_keys = lax.ppermute(keys, "ctx", CORE_SWAP)
     other_values = lax.ppermute(values, "ctx", CORE_SWAP)
     other_weight = lax.ppermute(out_weight, "ctx", CORE_SWAP)
 
     column = spread(queries, "ctx", Z_GROUPS).reshape(ZN * ROWS, WIDE)
+    cache = (keys, values, other_keys, other_values)
+    own = attend(True, hits, where, column.reshape(NQB, 16, WIDE), *cache)
     plane = spread(column, "ctx", X_GROUPS).reshape(XN, NQB, 16, WIDE)
-    states = attend(hits, core, plane, keys, values, other_keys, other_values)
+    states = attend(False, hits, where, plane, *cache, own=own)
     merged = merge(exchange(states, "ctx", X_GROUPS))
     arrived = exchange(merged.reshape(ZN, ROWS, STATE), "ctx", Z_GROUPS)
     attended = finish(arrived.reshape(ZN * ROWS, STATE)).reshape(ZN, ROWS, WIDE)

time: 150 us -> 139 us (0.927)
  waiting for transfers between devices: 38.9 us -> 32 us
  blocking collectives: 59.3 us -> 52.7 us
  local copies, waits for them, and re-layouts: 5.27 us -> 6.95 us
    all_to_all x4, waiting for transfers between devices: 38.9 us -> 31.9 us  [exchange(): lax.all_to_all(blocks, axis, split_axis=0, concat_axis=0, tiled=True, axi...]
    all_to_all x3, blocking collectives: 59.3 us -> 52.7 us  [exchange(): lax.all_to_all(blocks, axis, split_axis=0, concat_axis=0, tiled=True, axi...]
    unnamed x8 -> x12, local copies, waits for them, and re-layouts: 0.02 us -> 1.68 us
    pallas_call x1 -> x2, Pallas kernels: 13.8 us -> 15 us  [attend(): pl.pallas_call(functools.partial(attend_kernel, alone), name='attend_own'...]
  transfers between devices with their start and end apart: 7 -> 7, of which waited for: 4 -> 4; matrix products, arithmetic and copies ran while one was open for 2% -> 2% of each run, Pallas kernels for 0% -> 4%
where the time goes in v2:
time: 139 us
  blocking collectives  52.7 us (38%)
  waiting for transfers between devices  32 us (23%)
  starting transfers between devices  27.9 us (20%)
  Pallas kernels  18.5 us (13%)
  local copies, waits for them, and re-layouts  6.95 us (5%)
    all_to_all x3, blocking collectives, exchange(): lax.all_to_all(blocks, axis, split_axis=0, concat_axis=0, tiled=True, axi...  52.7 us
    all_to_all x4, waiting for transfers between devices, exchange(): lax.all_to_all(blocks, axis, split_axis=0, concat_axis=0, tiled=True, axi...  31.9 us
    all_to_all x4, starting transfers between devices, exchange(): lax.all_to_all(blocks, axis, split_axis=0, concat_axis=0, tiled=True, axi...  21.7 us
    pallas_call x2, Pallas kernels, attend(): pl.pallas_call(functools.partial(attend_kernel, alone), name='attend_own'...  15 us
    broadcast_in_dim x3, local copies, waits for them, and re-layouts, spread(): jnp.broadcast_to(rows[None], (count,) + rows.shape)  3.68 us
  transfers between devices with their start and end apart: 7, of which 4 were waited for; matrix products, arithmetic and copies ran while one was open for 2% of the time, Pallas kernels for 4%

profile of v2, /device:TPU:8, one launch (start us, length us, event | category | flops | bytes accessed | tf_op | source)
XLA Modules:
  0.0 138.6 jit_solution(17064344629392101822)
XLA Ops:
  0.0 0.0 copy-start
  0.0 1.5 %broadcast_in_dim.10 = bf16[8,8,2048]{2,1,0:T(8,128)(2,1)} broadcast(bf16[8,2048]{1,0:T(8,128)(2,1)} %param.6), dimensions={1,2} | broadcast | bytes 294912 | tf_op jit(solution)/shard_map/broadcast_in_dim | solution.py:51
  1.5 10.3 %all-to-all-start = ((bf16[8,8,2048]{2,1,0:T(8,128)(2,1)}), bf16[8,8,2048]{2,1,0:T(8,128)(2,1)S(1)}, u32[]{:S(2)}, u32[]{:S(2)}) async-start(bf16[8,8,2048]{2,1,0:T(8,128)(2,1)} %broadcast_in_dim.10), calls=%async_computation | async-start | bytes 524288 | tf_op jit(solution)/shard_map/all_to_all | solution.py:44
  11.8 1.9 %collective-permute-start = (bf16[4096,128]{1,0:T(8,128)(2,1)}, bf16[4096,128]{1,0:T(8,128)(2,1)}, u32[]{:S(2)}, u32[]{:S(2)}) collective-permute-start(bf16[4096,128]{1,0:T(8,128)(2,1)} %k0_ref.3), channel_id=1, source_target_pairs={{0,8},{8,0},{16,24},{24,16},{32,40},{40,32},{48,56},{56,48},{64,72... | collective-permute-start | bytes 3145736 | tf_op jit(solution)/shard_map/ppermute | solution.py:355
  13.7 2.4 %collective-permute-start.1 = (bf16[4096,128]{1,0:T(8,128)(2,1)}, bf16[4096,128]{1,0:T(8,128)(2,1)}, u32[]{:S(2)}, u32[]{:S(2)}) collective-permute-start(bf16[4096,128]{1,0:T(8,128)(2,1)} %v0_ref.3), channel_id=1, source_target_pairs={{0,8},{8,0},{16,24},{24,16},{32,40},{40,32},{48,56},{56,48},{64,72... | collective-permute-start | bytes 3145736 | tf_op jit(solution)/shard_map/ppermute | solution.py:356
  16.2 0.8 dynamic_slice.8
  16.9 0.1 reshape.43
  17.1 0.1 eq.35
  17.1 6.5 %all-to-all-done = bf16[8,8,2048]{2,1,0:T(8,128)(2,1)S(1)} async-done(((bf16[8,8,2048]{2,1,0:T(8,128)(2,1)}), bf16[8,8,2048]{2,1,0:T(8,128)(2,1)S(1)}, u32[]{:S(2)}, u32[]{:S(2)}) %all-to-all-start) | async-done | bytes 262176 | tf_op jit(solution)/shard_map/all_to_all | solution.py:44
  23.7 1.1 broadcast_in_dim.24
  24.8 0.0 copy-start.1
  24.8 0.0 copy-start.2
  24.8 4.4 %all-to-all-start.1 = ((bf16[4,64,2048]{2,1,0:T(8,128)(2,1)}), bf16[4,64,2048]{2,1,0:T(8,128)(2,1)S(1)}, u32[]{:S(2)}, u32[]{:S(2)}) async-start(bf16[4,64,2048]{2,1,0:T(8,128)(2,1)} %broadcast_in_dim.24), calls=%async_computation.1 | async-start | bytes 2097152 | tf_op jit(solution)/shard_map/all_to_all | solution.py:44
  29.2 0.1 pad_add_fusion.place_ref
  29.3 0.0 copy-done
  29.3 0.2 compare_reduce_fusion
  29.5 0.0 collective-permute-done.k1_ref
  29.5 0.0 collective-permute-done.1.v1_ref
  29.6 0.0 copy-done.1
  29.6 0.0 copy-done.2
  29.6 6.1 %attend_own.1.rest_0_ = bf16[64,2176]{1,0:T(8,128)(2,1)S(1)} custom-call(s32[4,16]{1,0:T(4,128)S(1)} %broadcast_select_fusion.hits_ref, s32[2]{0:T(128)S(1)} %pad_add_fusion.place_ref, bf16[4,16,2048]{2,1,0:T(8,128)(2,1)S(1)} %bitcast.18, bf16[4096,128]{1,0:T(8,128)(2,1)S(1)} %copy-done.1, bf16[4096,128]{1,0:T(8,128)(2,1)S(1)} %copy-done.2, ...), custom_call_target="tpu_custom_call" | custom-call | flops 536870912 | bytes 8388608 | tf_op jit(solution)/shard_map/attend_own/pallas_call | solution.py:219
  35.7 0.0 copy-start.3
  35.7 0.7 copy-done.3
  36.4 6.1 %all-to-all-done.1 = bf16[4,64,2048]{2,1,0:T(8,128)(2,1)S(1)} async-done(((bf16[4,64,2048]{2,1,0:T(8,128)(2,1)}), bf16[4,64,2048]{2,1,0:T(8,128)(2,1)S(1)}, u32[]{:S(2)}, u32[]{:S(2)}) %all-to-all-start.1) | async-done | bytes 1048608 | tf_op jit(solution)/shard_map/all_to_all | solution.py:44
  42.5 0.0 copy-start.4
  42.5 1.0 copy-done.4
  43.5 8.9 %attend_rest.1 = bf16[4,64,2176]{2,1,0:T(8,128)(2,1)} custom-call(s32[4,16]{1,0:T(4,128)S(1)} %broadcast_select_fusion.hits_ref, s32[2]{0:T(128)S(1)} %pad_add_fusion.place_ref, bf16[4,4,16,2048]{3,2,1,0:T(8,128)(2,1)S(1)} %bitcast.16, bf16[4096,128]{1,0:T(8,128)(2,1)S(1)} %copy-done.1, bf16[4096,128]{1,0:T(8,128)(2,1)S(1)} %copy-done.2, ...), custom_call_target="tpu_custom_call" | custom-call | flops 1610612736 | bytes 8388608 | tf_op jit(solution)/shard_map/attend_rest/pallas_call | solution.py:219
  52.4 18.0 %all_to_all.35.in_ref = bf16[4,64,2176]{2,1,0:T(8,128)(2,1)S(1)} all-to-all(bf16[4,64,2176]{2,1,0:T(8,128)(2,1)} %attend_rest.1), channel_id=1, replica_groups={{0,16,32,48},{8,24,40,56},{64,80,96,112},{72,88,104,120},{128,144,160,1..., dimensions={0} | all-to-all | bytes 2228224 | tf_op jit(solution)/shard_map/all_to_all | solution.py:44
  70.3 1.7 %shard_map.64 = bf16[64,2176]{1,0:T(8,128)(2,1)S(1)} custom-call(bf16[4,64,2176]{2,1,0:T(8,128)(2,1)S(1)} %all_to_all.35.in_ref), custom_call_target="tpu_custom_call" | custom-call | tf_op jit(solution)/shard_map/pallas_call | solution.py:273
  72.1 0.0 copy-start.5
  72.1 17.2 %all_to_all.36 = bf16[8,8,2176]{2,1,0:T(8,128)(2,1)S(1)} all-to-all(bf16[8,8,2176]{2,1,0:T(8,128)(2,1)S(1)} %bitcast.19), channel_id=1, replica_groups={{0,64,128,192,256,320,384,448},{8,72,136,200,264,328,392,456},{16,80,14..., dimensions={0} | all-to-all | bytes 557056 | tf_op jit(solution)/shard_map/all_to_all | solution.py:44
  89.2 1.1 shard_map.65
  90.3 3.4 %all-to-all-start.4 = ((bf16[8,8,2048]{2,1,0:T(8,128)(2,1)}), bf16[8,8,2048]{2,1,0:T(8,128)(2,1)S(1)}, u32[]{:S(2)}, u32[]{:S(2)}) async-start(bf16[8,8,2048]{2,1,0:T(8,128)(2,1)} %bitcast.8), calls=%async_computation.4 | async-start | bytes 524288 | tf_op jit(solution)/shard_map/all_to_all | solution.py:44
  93.8 0.0 copy-done.5
  93.8 1.9 %collective-permute-start.2 = (bf16[2048,256]{1,0:T(8,128)(2,1)S(1)}, bf16[2048,256]{1,0:T(8,128)(2,1)S(1)}, u32[]{:S(2)}, u32[]{:S(2)}) collective-permute-start(bf16[2048,256]{1,0:T(8,128)(2,1)S(1)} %copy-done.5), channel_id=1, source_target_pairs={{0,8},{8,0},{16,24},{24,16},{32,40},{40,32},{48,56},{56,48},{64,72... | collective-permute-start | bytes 3145736 | tf_op jit(solution)/shard_map/ppermute | solution.py:357
  95.7 8.5 %all-to-all-done.4 = bf16[8,8,2048]{2,1,0:T(8,128)(2,1)S(1)} async-done(((bf16[8,8,2048]{2,1,0:T(8,128)(2,1)}), bf16[8,8,2048]{2,1,0:T(8,128)(2,1)S(1)}, u32[]{:S(2)}, u32[]{:S(2)}) %all-to-all-start.4) | async-done | bytes 262176 | tf_op jit(solution)/shard_map/all_to_all | solution.py:44
  104.2 1.1 broadcast_in_dim.26
  105.2 3.5 %all-to-all-start.5 = ((bf16[4,64,2048]{2,1,0:T(8,128)(2,1)}), bf16[4,64,2048]{2,1,0:T(8,128)(2,1)S(1)}, u32[]{:S(2)}, u32[]{:S(2)}) async-start(bf16[4,64,2048]{2,1,0:T(8,128)(2,1)} %broadcast_in_dim.26), calls=%async_computation.5 | async-start | bytes 2097152 | tf_op jit(solution)/shard_map/all_to_all | solution.py:44
  108.8 0.0 collective-permute-done.2.w1_ref
  108.8 10.8 %all-to-all-done.5.a_ref = bf16[4,64,2048]{2,1,0:T(8,128)(2,1)S(1)} async-done(((bf16[4,64,2048]{2,1,0:T(8,128)(2,1)}), bf16[4,64,2048]{2,1,0:T(8,128)(2,1)S(1)}, u32[]{:S(2)}, u32[]{:S(2)}) %all-to-all-start.5) | async-done | bytes 1048608 | tf_op jit(solution)/shard_map/all_to_all | solution.py:44
  119.6 0.7 shard_map.66
  120.3 17.6 %all_to_all.37 = bf16[16,32,256]{2,1,0:T(8,128)(2,1)S(1)} all-to-all(bf16[16,32,256]{2,1,0:T(8,128)(2,1)S(1)} %bitcast.21), channel_id=1, replica_groups={{0,1,2,3,4,5,6,7,8,9,10,11,12,13,14,15},{16,17,18,19,20,21,22,23,24,25,..., dimensions={0} | all-to-all | bytes 524288 | tf_op jit(solution)/shard_map/all_to_all | solution.py:44
  138.0 0.6 copy.8
  (6 shorter events, 0.1 us)
Async XLA Ops:
  0.0 29.3 %copy-start = (s32[8,4,64]{2,1,0:T(4,128)S(1)}, s32[8,4,64]{2,1,0:T(4,128)}, u32[]{:S(2)}) copy-start(s32[8,4,64]{2,1,0:T(4,128)} %param.10) | copy-start | bytes 24580
  1.5 22.2 %all-to-all-start = ((bf16[8,8,2048]{2,1,0:T(8,128)(2,1)}), bf16[8,8,2048]{2,1,0:T(8,128)(2,1)S(1)}, u32[]{:S(2)}, u32[]{:S(2)}) async-start(bf16[8,8,2048]{2,1,0:T(8,128)(2,1)} %broadcast_in_dim.10), calls=%async_computation | async-start | bytes 524288 | tf_op jit(solution)/shard_map/all_to_all | solution.py:44
  11.8 17.7 %collective-permute-start = (bf16[4096,128]{1,0:T(8,128)(2,1)}, bf16[4096,128]{1,0:T(8,128)(2,1)}, u32[]{:S(2)}, u32[]{:S(2)}) collective-permute-start(bf16[4096,128]{1,0:T(8,128)(2,1)} %k0_ref.3), channel_id=1, source_target_pairs={{0,8},{8,0},{16,24},{24,16},{32,40},{40,32},{48,56},{56,48},{64,72... | collective-permute-start | bytes 3145736 | tf_op jit(solution)/shard_map/ppermute | solution.py:355
  13.7 15.8 %collective-permute-start.1 = (bf16[4096,128]{1,0:T(8,128)(2,1)}, bf16[4096,128]{1,0:T(8,128)(2,1)}, u32[]{:S(2)}, u32[]{:S(2)}) collective-permute-start(bf16[4096,128]{1,0:T(8,128)(2,1)} %v0_ref.3), channel_id=1, source_target_pairs={{0,8},{8,0},{16,24},{24,16},{32,40},{40,32},{48,56},{56,48},{64,72... | collective-permute-start | bytes 3145736 | tf_op jit(solution)/shard_map/ppermute | solution.py:356
  24.8 4.8 %copy-start.1 = (bf16[4096,128]{1,0:T(8,128)(2,1)S(1)}, bf16[4096,128]{1,0:T(8,128)(2,1)}, u32[]{:S(2)}) copy-start(bf16[4096,128]{1,0:T(8,128)(2,1)} %k0_ref.3) | copy-start | bytes 3145732
  24.8 4.8 %copy-start.2 = (bf16[4096,128]{1,0:T(8,128)(2,1)S(1)}, bf16[4096,128]{1,0:T(8,128)(2,1)}, u32[]{:S(2)}) copy-start(bf16[4096,128]{1,0:T(8,128)(2,1)} %v0_ref.3) | copy-start | bytes 3145732
  24.8 17.7 %all-to-all-start.1 = ((bf16[4,64,2048]{2,1,0:T(8,128)(2,1)}), bf16[4,64,2048]{2,1,0:T(8,128)(2,1)S(1)}, u32[]{:S(2)}, u32[]{:S(2)}) async-start(bf16[4,64,2048]{2,1,0:T(8,128)(2,1)} %broadcast_in_dim.24), calls=%async_computation.1 | async-start | bytes 2097152 | tf_op jit(solution)/shard_map/all_to_all | solution.py:44
  35.7 0.7 copy-start.3
  42.5 1.0 copy-start.4
  72.1 21.7 %copy-start.5 = (bf16[2048,256]{1,0:T(8,128)(2,1)S(1)}, bf16[2048,256]{1,0:T(8,128)(2,1)}, u32[]{:S(2)}) copy-start(bf16[2048,256]{1,0:T(8,128)(2,1)} %w0_ref.1) | copy-start | bytes 3145732
  90.3 13.8 %all-to-all-start.4 = ((bf16[8,8,2048]{2,1,0:T(8,128)(2,1)}), bf16[8,8,2048]{2,1,0:T(8,128)(2,1)S(1)}, u32[]{:S(2)}, u32[]{:S(2)}) async-start(bf16[8,8,2048]{2,1,0:T(8,128)(2,1)} %bitcast.8), calls=%async_computation.4 | async-start | bytes 524288 | tf_op jit(solution)/shard_map/all_to_all | solution.py:44
  93.8 15.0 %collective-permute-start.2 = (bf16[2048,256]{1,0:T(8,128)(2,1)S(1)}, bf16[2048,256]{1,0:T(8,128)(2,1)S(1)}, u32[]{:S(2)}, u32[]{:S(2)}) collective-permute-start(bf16[2048,256]{1,0:T(8,128)(2,1)S(1)} %copy-done.5), channel_id=1, source_target_pairs={{0,8},{8,0},{16,24},{24,16},{32,40},{40,32},{48,56},{56,48},{64,72... | collective-permute-start | bytes 3145736 | tf_op jit(solution)/shard_map/ppermute | solution.py:357
  105.2 14.4 %all-to-all-start.5 = ((bf16[4,64,2048]{2,1,0:T(8,128)(2,1)}), bf16[4,64,2048]{2,1,0:T(8,128)(2,1)S(1)}, u32[]{:S(2)}, u32[]{:S(2)}) async-start(bf16[4,64,2048]{2,1,0:T(8,128)(2,1)} %broadcast_in_dim.26), calls=%async_computation.5 | async-start | bytes 2097152 | tf_op jit(solution)/shard_map/all_to_all | solution.py:44

commit v3 on v2

--- a/solution.py
+++ b/solution.py
@@ -21,7 +21,7 @@
 STATE = WIDE + 128
 SCALE = math.log2(math.e) / math.sqrt(DH)
 NEG = -(2.0**100)
-VMEM_LIMIT = 48 * 1024 * 1024
+VMEM_LIMIT = 24 * 1024 * 1024
 F32 = jnp.float32
 BF16 = jnp.bfloat16
 
@@ -32,6 +32,17 @@
 
 Z_GROUPS = [[place(z, x, c) for z in range(ZN)] for x in range(XN) for c in range(2)]
 X_GROUPS = [[place(z, x, c) for x in range(XN)] for z in range(ZN) for c in range(2)]
+NEAR_GROUPS = [
+    [place((2 * pair + low + c) % ZN, x, c) for low in range(2) for x in range(XN)]
+    for pair in range(ZN // 2)
+    for c in range(2)
+]
+FAR_GROUPS = [
+    [place((2 * pair + low + c) % ZN, x, c) for pair in range(ZN // 2)]
+    for low in range(2)
+    for x in range(XN)
+    for c in range(2)
+]
 YC_GROUPS = [
     [place(z, x, c) * YN + y for c in range(2) for y in range(YN)]
     for z in range(ZN)
@@ -55,29 +66,27 @@
     return pl.BlockSpec(memory_space=pltpu.VMEM)
 
 
+def in_hbm():
+    return pl.BlockSpec(memory_space=pltpu.HBM)
+
+
 def in_smem():
     return pl.BlockSpec(memory_space=pltpu.SMEM)
 
 
-def attend_kernel(
-    alone,
-    hits_ref,
-    place_ref,
-    q_ref,
-    k0_ref,
-    v0_ref,
-    k1_ref,
-    v1_ref,
-    *rest,
-):
-    own_ref = None if alone else rest[0]
-    out_ref, top, total, acc, scaled, k_all, v_all, listed, sems = rest[0 if alone else 1 :]
+def attend_kernel(alone, place_ref, q_ref, *rest):
     tile = GROUP * 16
+    column = place_ref[0]
+    core = place_ref[1]
+    if alone:
+        hits_ref, k0_ref, v0_ref, k1_ref, v1_ref, final_ref, listed, out_ref = rest[:8]
+        parts = [column]
+    else:
+        listed, k0_ref, v0_ref, k1_ref, v1_ref, out_ref = rest[:6]
+        parts = [lax.rem(column + j, XN) for j in range(1, XN)]
+    top, total, acc, scaled, k_all, v_all, sems = rest[8 if alone else 6 :]
     local = k0_ref.shape[0]
     blocks = 2 * local // BLKSZ
-    column = place_ref[0]
-    core = place_ref[1]
-    parts = [column] if alone else [lax.rem(column + j, XN) for j in range(1, XN)]
     copies = []
     for i, (source, target, start) in enumerate(
         ((k0_ref, k_all, 0), (v0_ref, v_all, 0), (k1_ref, k_all, local), (v1_ref, v_all, local))
@@ -85,10 +94,26 @@
         copy = pltpu.make_async_copy(source, target.at[pl.ds(start, local)], sems.at[i])
         copy.start()
         copies.append(copy)
-    if not alone:
-        out_ref[column] = own_ref[...]
-    for copy in copies:
-        copy.wait()
+
+    if alone:
+
+        def collect(c, carry):
+            listed[c, blocks + 1] = -1
+
+            def look(b, found):
+                kind = hits_ref[c, b]
+                listed[c, found] = b
+
+                @pl.when(kind == 2)
+                def _():
+                    listed[c, blocks + 1] = b
+
+                return found + jnp.where(kind == 1, 1, 0)
+
+            listed[c, blocks] = lax.fori_loop(0, blocks, look, 0)
+            return carry
+
+        lax.fori_loop(0, NQB, collect, 0)
 
     def block_of(ref, b):
         return ref[pl.ds(pl.multiple_of(b * BLKSZ, BLKSZ), BLKSZ), :]
@@ -137,7 +162,7 @@
             scores = following
         gather(*before)
 
-    def query_block(c, carry):
+    def prepare(c):
         top[...] = jnp.full(top.shape, NEG, F32)
         total[...] = jnp.zeros(total.shape, F32)
         acc[...] = jnp.zeros(acc.shape, F32)
@@ -149,15 +174,17 @@
             low = (rows - high.astype(F32)).astype(BF16)
             scaled[rows_of(i)] = jnp.concatenate([high, low], axis=1)
 
-        def collect(b, found):
-            listed[found] = b
-            return found + jnp.where(hits_ref[c, b] == 1, 1, 0)
-
-        found = lax.fori_loop(0, blocks, collect, 0)
+    def query_block(c, carry):
+        @pl.when(c > 0)
+        def _():
+            prepare(c)
+
+        found = listed[c, blocks]
+        current = listed[c, blocks + 1]
         span = range(len(parts))
 
         def two(j, carry):
-            first, second = listed[2 * j], listed[2 * j + 1]
+            first, second = listed[c, 2 * j], listed[c, 2 * j + 1]
             if alone:
                 run([(i, [b]) for b in (first, second) for i in span])
             else:
@@ -168,21 +195,16 @@
 
         @pl.when(found % 2 == 1)
         def _():
-            run([(i, [listed[found - 1]]) for i in span])
-
-        def current(b, carry):
-            @pl.when(hits_ref[c, b] == 2)
-            def _():
-                def mask(i):
-                    row = lax.broadcasted_iota(jnp.int32, (tile, BLKSZ), 0) % 16
-                    token = (((2 * c + row // 8) * XN + parts[i]) * 2 + core) * ROWS + row % 8
-                    return lax.broadcasted_iota(jnp.int32, (tile, BLKSZ), 1) <= token
-
-                run([(i, [b]) for i in span], mask)
-
-            return carry
-
-        lax.fori_loop(0, blocks, current, 0)
+            run([(i, [listed[c, found - 1]]) for i in span])
+
+        @pl.when(current >= 0)
+        def _():
+            def mask(i):
+                row = lax.broadcasted_iota(jnp.int32, (tile, BLKSZ), 0) % 16
+                token = (((2 * c + row // 8) * XN + parts[i]) * 2 + core) * ROWS + row % 8
+                return lax.broadcasted_iota(jnp.int32, (tile, BLKSZ), 1) <= token
+
+            run([(i, [current]) for i in span], mask)
 
         first = pl.multiple_of(c * 16, 16)
         lane = lax.broadcasted_iota(jnp.int32, (16, 128), 1)
@@ -205,38 +227,60 @@
             target[pl.ds(first, 16), WIDE:] = stats.astype(BF16)
         return carry
 
+    prepare(0)
+    for copy in copies:
+        copy.wait()
     lax.fori_loop(0, NQB, query_block, 0)
-
-
-def attend(alone, hits, where, q, k0, v0, k1, v1, own=None):
-    parts = 1 if alone else XN - 1
-    tile = GROUP * 16
-    shape = (NQB * 16, STATE) if alone else (XN, NQB * 16, STATE)
-    operands = (hits, where, q, k0, v0, k1, v1) + (() if alone else (own,))
-    specs = [in_smem(), in_smem(), in_vmem()] + [pl.BlockSpec(memory_space=pl.ANY)] * 4
-    specs += [] if alone else [in_vmem()]
-    pairs = 8 * parts * tile * BLKSZ
+    if alone:
+        copy = pltpu.make_async_copy(out_ref, final_ref, sems.at[4])
+        copy.start()
+        copy.wait()
+
+
+def state_scratch(parts, tokens):
+    tile = parts * GROUP * 16
+    return [
+        pltpu.VMEM((tile, 128), F32),
+        pltpu.VMEM((tile, 128), F32),
+        pltpu.VMEM((tile, DH), F32),
+        pltpu.VMEM((tile, 2 * DH), BF16),
+        pltpu.VMEM((tokens, DH), BF16),
+        pltpu.VMEM((tokens, DH), BF16),
+        pltpu.SemaphoreType.DMA((5,)),
+    ]
+
+
+def attend_cost(parts):
+    pairs = 8 * parts * GROUP * 16 * BLKSZ
+    return pl.CostEstimate(flops=pairs * 4 * DH, bytes_accessed=8 * 1024 * 1024, transcendentals=pairs)
+
+
+def attend_own(where, q, hits, cache):
+    tokens = 2 * cache[0].shape[0]
+    state = jax.ShapeDtypeStruct((NQB * 16, STATE), BF16)
     return pl.pallas_call(
-        functools.partial(attend_kernel, alone),
-        name="attend_own" if alone else "attend_rest",
-        out_shape=jax.ShapeDtypeStruct(shape, BF16),
-        in_specs=specs,
+        functools.partial(attend_kernel, True),
+        name="attend_own",
+        out_shape=(state, jax.ShapeDtypeStruct((NQB, tokens // BLKSZ + 8), jnp.int32)),
+        in_specs=[in_smem(), in_vmem(), in_smem()] + [in_hbm()] * 4,
+        out_specs=(in_hbm(), in_smem()),
+        scratch_shapes=[pltpu.VMEM(state.shape, BF16)] + state_scratch(1, tokens),
+        compiler_params=pltpu.CompilerParams(vmem_limit_bytes=VMEM_LIMIT),
+        cost_estimate=attend_cost(1),
+    )(where, q, hits, *cache)
+
+
+def attend_rest(where, q, listed, cache):
+    return pl.pallas_call(
+        functools.partial(attend_kernel, False),
+        name="attend_rest",
+        out_shape=jax.ShapeDtypeStruct((XN, NQB * 16, STATE), BF16),
+        in_specs=[in_smem(), in_vmem(), in_smem()] + [in_hbm()] * 4,
         out_specs=in_vmem(),
-        scratch_shapes=[
-            pltpu.VMEM((parts * tile, 128), F32),
-            pltpu.VMEM((parts * tile, 128), F32),
-            pltpu.VMEM((parts * tile, DH), F32),
-            pltpu.VMEM((parts * tile, 2 * DH), BF16),
-            pltpu.VMEM((2 * k0.shape[0], DH), BF16),
-            pltpu.VMEM((2 * k0.shape[0], DH), BF16),
-            pltpu.SMEM((2 * k0.shape[0] // BLKSZ + 8,), jnp.int32),
-            pltpu.SemaphoreType.DMA((4,)),
-        ],
+        scratch_shapes=state_scratch(XN - 1, 2 * cache[0].shape[0]),
         compiler_params=pltpu.CompilerParams(vmem_limit_bytes=VMEM_LIMIT),
-        cost_estimate=pl.CostEstimate(
-            flops=pairs * 4 * DH, bytes_accessed=8 * 1024 * 1024, transcendentals=pairs
-        ),
-    )(*operands)
+        cost_estimate=attend_cost(XN - 1),
+    )(where, q, listed, *cache)
 
 
 def weights_of(stats):
@@ -252,31 +296,32 @@
     return peak, weights, total
 
 
-def merge_kernel(in_ref, out_ref):
-    count, rows = in_ref.shape[0], in_ref.shape[1]
-    for r in range(0, rows, 16):
-        stats = [in_ref[s, r : r + 16, WIDE:].astype(F32) for s in range(count)]
-        peak, weights, total = weights_of(stats)
-        for h in range(GROUP):
-            cols = slice(h * DH, (h + 1) * DH)
-            value = None
-            for s in range(count):
-                term = in_ref[s, r : r + 16, cols].astype(F32) * weights[s][:, h : h + 1]
-                value = term if value is None else value + term
-            out_ref[r : r + 16, cols] = value.astype(BF16)
-        high = total.astype(BF16).astype(F32)
-        rest = jnp.zeros((16, 128 - 3 * GROUP), F32)
-        out_ref[r : r + 16, WIDE:] = jnp.concatenate([peak, high, total - high, rest], axis=1).astype(BF16)
-
-
-def merge(states):
+def merge_kernel(place_ref, own_ref, in_ref, out_ref):
+    rows = own_ref.shape[0]
+    column = place_ref[0]
+    sources = [own_ref] + [in_ref.at[lax.rem(column + j, XN)] for j in range(1, XN)]
+    peak, weights, total = weights_of([s[:, WIDE:].astype(F32) for s in sources])
+    for h in range(GROUP):
+        cols = slice(h * DH, (h + 1) * DH)
+        value = None
+        for source, weight in zip(sources, weights):
+            term = source[:, cols].astype(F32) * weight[:, h : h + 1]
+            value = term if value is None else value + term
+        out_ref[:, cols] = value.astype(BF16)
+    high = total.astype(BF16).astype(F32)
+    rest = jnp.zeros((rows, 128 - 3 * GROUP), F32)
+    out_ref[:, WIDE:] = jnp.concatenate([peak, high, total - high, rest], axis=1).astype(BF16)
+
+
+def merge(where, own, states):
     return pl.pallas_call(
         merge_kernel,
+        name="merge",
         out_shape=jax.ShapeDtypeStruct(states.shape[1:], BF16),
-        in_specs=[in_vmem()],
+        in_specs=[in_smem(), in_vmem(), in_vmem()],
         out_specs=in_vmem(),
         compiler_params=pltpu.CompilerParams(vmem_limit_bytes=VMEM_LIMIT),
-    )(states)
+    )(where, own, states)
 
 
 def finish_kernel(in_ref, out_ref):
@@ -299,14 +344,14 @@
             )
             value = term if value is None else value + term
         twice = jnp.concatenate([value, value], axis=0).astype(BF16)
-        for i in range(pairs):
+        for i in range(out_ref.shape[0] // 16):
             out_ref[i * 16 : (i + 1) * 16, cols] = twice
 
 
 def finish(states):
     return pl.pallas_call(
         finish_kernel,
-        out_shape=jax.ShapeDtypeStruct((ZN * ROWS, WIDE), BF16),
+        out_shape=jax.ShapeDtypeStruct((ZN // 2 * ROWS, WIDE), BF16),
         in_specs=[in_vmem()],
         out_specs=in_vmem(),
         compiler_params=pltpu.CompilerParams(vmem_limit_bytes=VMEM_LIMIT),
@@ -319,11 +364,11 @@
     for side, w_ref in enumerate((w0_ref, w1_ref)):
         result = jnp.dot(rows, w_ref[...], preferred_element_type=F32)
         target = core if side == 0 else 1 - core
-        for z in range(ZN):
-            chunk = jnp.concatenate(
-                [result[(x * ZN + z) * ROWS : (x * ZN + z + 1) * ROWS] for x in range(XN)], axis=0
-            )
-            out_ref[target, z] = chunk.astype(BF16)
+        for w in range(ZN):
+            pair, low = w // 2, w % 2
+            starts = [((low * XN + x) * (ZN // 2) + pair) * ROWS for x in range(XN)]
+            chunk = jnp.concatenate([result[start : start + ROWS] for start in starts], axis=0)
+            out_ref[target, lax.rem(w + core, ZN)] = chunk.astype(BF16)
 
 
 def project(core, rows, w0, w1):
@@ -354,19 +399,20 @@
     hits = find_hits(block_slots, selected, device, head, keys.shape[0] // BLKSZ)
     other_keys = lax.ppermute(keys, "ctx", CORE_SWAP)
     other_values = lax.ppermute(values, "ctx", CORE_SWAP)
-    other_weight = lax.ppermute(out_weight, "ctx", CORE_SWAP)
 
     column = spread(queries, "ctx", Z_GROUPS).reshape(ZN * ROWS, WIDE)
     cache = (keys, values, other_keys, other_values)
-    own = attend(True, hits, where, column.reshape(NQB, 16, WIDE), *cache)
+    own, listed = attend_own(where, column.reshape(NQB, 16, WIDE), hits, cache)
     plane = spread(column, "ctx", X_GROUPS).reshape(XN, NQB, 16, WIDE)
-    states = attend(False, hits, where, plane, *cache, own=own)
-    merged = merge(exchange(states, "ctx", X_GROUPS))
+    states = attend_rest(where, plane, listed, cache)
+    states, out_weight = lax.optimization_barrier((states, out_weight))
+    other_weight = lax.ppermute(out_weight, "ctx", CORE_SWAP)
+    merged = merge(where, own, exchange(states, "ctx", X_GROUPS))
     arrived = exchange(merged.reshape(ZN, ROWS, STATE), "ctx", Z_GROUPS)
-    attended = finish(arrived.reshape(ZN * ROWS, STATE)).reshape(ZN, ROWS, WIDE)
-
-    column = exchange(attended, "ctx", Z_GROUPS).reshape(ZN * ROWS, WIDE)
-    plane = spread(column, "ctx", X_GROUPS)
+    attended = finish(arrived.reshape(ZN * ROWS, STATE)).reshape(ZN // 2, ROWS, WIDE)
+
+    column = exchange(attended, "ctx", FAR_GROUPS).reshape(ZN // 2 * ROWS, WIDE)
+    plane = spread(column, "ctx", NEAR_GROUPS)
     shares = project(core, plane, out_weight, other_weight)
     arrived = exchange(shares.reshape(2 * YN, XN * ROWS, -1), ("ctx", "kvh"), YC_GROUPS)
     summed = jnp.sum(arrived.reshape(2, YN, XN, ROWS, -1).astype(F32), axis=1)

time: 139 us -> 135 us (0.971)
  blocking collectives: 52.7 us -> 64.8 us
  waiting for transfers between devices: 32 us -> 21 us
  starting transfers between devices: 27.9 us -> 24.7 us
  Pallas kernels: 18.5 us -> 16.7 us
    all_to_all x4 -> x3, waiting for transfers between devices: 31.9 us -> 18.4 us  [exchange(): lax.all_to_all(blocks, axis, split_axis=0, concat_axis=0, tiled=True, axi...]
    all_to_all x3 -> x4, blocking collectives: 52.7 us -> 64.8 us  [exchange(): lax.all_to_all(blocks, axis, split_axis=0, concat_axis=0, tiled=True, axi...]
    all_to_all x4 -> x3, starting transfers between devices: 21.7 us -> 18.4 us  [exchange(): lax.all_to_all(blocks, axis, split_axis=0, concat_axis=0, tiled=True, axi...]
    ppermute x1, waiting for transfers between devices: 0.01 us -> 2.63 us  [body(): other_weight = lax.ppermute(out_weight, 'ctx', CORE_SWAP)]
    pallas_call x4, Pallas kernels: 17.8 us -> 16 us  [the longest x1 8.07 us: attend_rest(): pl.pallas_call(functools.partial(attend_kernel, False), name='attend_rest...]
  transfers between devices with their start and end apart: 7 -> 6, of which waited for: 4 -> 4; matrix products, arithmetic and copies ran while one was open for 2% -> 2% of each run, Pallas kernels for 4% -> 5%
where the time goes in v3:
time: 135 us; the launch traced here: 134 us
  blocking collectives  64.8 us (48%)
  starting transfers between devices  24.7 us (18%)
  waiting for transfers between devices  21 us (16%)
  Pallas kernels  16.7 us (12%)
  local copies, waits for them, and re-layouts  6.01 us (4%)
    all_to_all x4, blocking collectives, exchange(): lax.all_to_all(blocks, axis, split_axis=0, concat_axis=0, tiled=True, axi...  64.8 us
    all_to_all x3, starting transfers between devices, exchange(): lax.all_to_all(blocks, axis, split_axis=0, concat_axis=0, tiled=True, axi...  18.4 us
    all_to_all x3, waiting for transfers between devices, exchange(): lax.all_to_all(blocks, axis, split_axis=0, concat_axis=0, tiled=True, axi...  18.4 us
    pallas_call x1, Pallas kernels, attend_rest(): pl.pallas_call(functools.partial(attend_kernel, False), name='attend_rest...  8.07 us
    pallas_call x1, Pallas kernels, attend_own(): pl.pallas_call(functools.partial(attend_kernel, True), name='attend_own',...  6.31 us
    broadcast_in_dim x3, local copies, waits for them, and re-layouts, spread(): jnp.broadcast_to(rows[None], (count,) + rows.shape)  3.69 us
  transfers between devices with their start and end apart: 6, of which 4 were waited for; matrix products, arithmetic and copies ran while one was open for 2% of the time, Pallas kernels for 5%

profile of v3, /device:TPU:8, one launch (start us, length us, event | category | flops | bytes accessed | tf_op | source)
XLA Modules:
  0.0 133.8 jit_solution(1613415731330853006)
XLA Ops:
  0.0 0.0 copy-start
  0.0 1.5 %broadcast_in_dim.10 = bf16[8,8,2048]{2,1,0:T(8,128)(2,1)} broadcast(bf16[8,2048]{1,0:T(8,128)(2,1)} %param.6), dimensions={1,2} | broadcast | bytes 294912 | tf_op jit(solution)/shard_map/broadcast_in_dim | solution.py:62
  1.5 10.3 %all-to-all-start = ((bf16[8,8,2048]{2,1,0:T(8,128)(2,1)}), bf16[8,8,2048]{2,1,0:T(8,128)(2,1)S(1)}, u32[]{:S(2)}, u32[]{:S(2)}) async-start(bf16[8,8,2048]{2,1,0:T(8,128)(2,1)} %broadcast_in_dim.10), calls=%async_computation | async-start | bytes 524288 | tf_op jit(solution)/shard_map/all_to_all | solution.py:55
  11.8 1.9 %collective-permute-start = (bf16[4096,128]{1,0:T(8,128)(2,1)}, bf16[4096,128]{1,0:T(8,128)(2,1)}, u32[]{:S(2)}, u32[]{:S(2)}) collective-permute-start(bf16[4096,128]{1,0:T(8,128)(2,1)} %rest_1_.3), channel_id=1, source_target_pairs={{0,8},{8,0},{16,24},{24,16},{32,40},{40,32},{48,56},{56,48},{64,72... | collective-permute-start | bytes 3145736 | tf_op jit(solution)/shard_map/ppermute | solution.py:400
  13.7 2.4 %collective-permute-start.1 = (bf16[4096,128]{1,0:T(8,128)(2,1)}, bf16[4096,128]{1,0:T(8,128)(2,1)}, u32[]{:S(2)}, u32[]{:S(2)}) collective-permute-start(bf16[4096,128]{1,0:T(8,128)(2,1)} %rest_2_.3), channel_id=1, source_target_pairs={{0,8},{8,0},{16,24},{24,16},{32,40},{40,32},{48,56},{56,48},{64,72... | collective-permute-start | bytes 3145736 | tf_op jit(solution)/shard_map/ppermute | solution.py:401
  16.2 0.8 dynamic_slice.8
  16.9 0.1 reshape.43
  17.1 0.1 eq.35
  17.1 6.5 %all-to-all-done = bf16[8,8,2048]{2,1,0:T(8,128)(2,1)S(1)} async-done(((bf16[8,8,2048]{2,1,0:T(8,128)(2,1)}), bf16[8,8,2048]{2,1,0:T(8,128)(2,1)S(1)}, u32[]{:S(2)}, u32[]{:S(2)}) %all-to-all-start) | async-done | bytes 262176 | tf_op jit(solution)/shard_map/all_to_all | solution.py:55
  23.7 1.1 broadcast_in_dim.24
  24.8 0.0 copy-start.1
  24.8 0.0 copy-start.2
  24.8 4.4 %all-to-all-start.1 = ((bf16[4,64,2048]{2,1,0:T(8,128)(2,1)}), bf16[4,64,2048]{2,1,0:T(8,128)(2,1)S(1)}, u32[]{:S(2)}, u32[]{:S(2)}) async-start(bf16[4,64,2048]{2,1,0:T(8,128)(2,1)} %broadcast_in_dim.24), calls=%async_computation.1 | async-start | bytes 2097152 | tf_op jit(solution)/shard_map/all_to_all | solution.py:55
  29.2 0.1 pad_add_fusion.place_ref
  29.3 0.0 copy-done
  29.3 0.2 compare_reduce_fusion
  29.5 0.0 collective-permute-done.rest_3_
  29.6 0.0 collective-permute-done.1.rest_4_
  29.6 0.0 copy-done.1
  29.6 0.0 copy-done.2
  29.6 6.3 %attend_own.1 = (bf16[64,2176]{1,0:T(8,128)(2,1)S(1)}, s32[4,24]{1,0:T(4,128)S(1)}) custom-call(s32[2]{0:T(128)S(1)} %pad_add_fusion.place_ref, bf16[4,16,2048]{2,1,0:T(8,128)(2,1)S(1)} %bitcast.18, s32[4,16]{1,0:T(4,128)S(1)} %broadcast_select_fusion.rest_0_, bf16[4096,128]{1,0:T(8,128)(2,1)S(1)} %copy-done.1, bf16[4096,128]{1,0:T(8,128)(2,1)S(1)} %copy-done.2, ...), custom_call_target="tpu_custom_call" | custom-call | flops 536870912 | bytes 8388608 | tf_op jit(solution)/shard_map/attend_own/pallas_call | solution.py:261
  35.9 0.0 copy-start.4
  35.9 0.7 copy-done.4
  36.6 5.9 %all-to-all-done.1 = bf16[4,64,2048]{2,1,0:T(8,128)(2,1)S(1)} async-done(((bf16[4,64,2048]{2,1,0:T(8,128)(2,1)}), bf16[4,64,2048]{2,1,0:T(8,128)(2,1)S(1)}, u32[]{:S(2)}, u32[]{:S(2)}) %all-to-all-start.1) | async-done | bytes 1048608 | tf_op jit(solution)/shard_map/all_to_all | solution.py:55
  42.5 8.1 %attend_rest.1 = bf16[4,64,2176]{2,1,0:T(8,128)(2,1)S(1)} custom-call(s32[2]{0:T(128)S(1)} %pad_add_fusion.place_ref, bf16[4,4,16,2048]{3,2,1,0:T(8,128)(2,1)S(1)} %bitcast.16, s32[4,24]{1,0:T(4,128)S(1)} %get-tuple-element.10.rest_0_, bf16[4096,128]{1,0:T(8,128)(2,1)S(1)} %copy-done.1, bf16[4096,128]{1,0:T(8,128)(2,1)S(1)} %copy-done.2, ...), custom_call_target="tpu_custom_call" | custom-call | flops 1610612736 | bytes 8388608 | tf_op jit(solution)/shard_map/attend_rest/pallas_call | solution.py:274
  50.6 0.0 copy-start.5
  50.6 17.3 %all_to_all.35.in_ref = bf16[4,64,2176]{2,1,0:T(8,128)(2,1)S(1)} all-to-all(bf16[4,64,2176]{2,1,0:T(8,128)(2,1)S(1)} %attend_rest.1), channel_id=1, replica_groups={{0,16,32,48},{8,24,40,56},{64,80,96,112},{72,88,104,120},{128,144,160,1..., dimensions={0} | all-to-all | bytes 2228224 | tf_op jit(solution)/shard_map/all_to_all | solution.py:55
  67.9 0.0 copy-done.5
  67.9 1.3 merge.1
  69.2 16.1 %all_to_all.36 = bf16[8,8,2176]{2,1,0:T(8,128)(2,1)S(1)} all-to-all(bf16[8,8,2176]{2,1,0:T(8,128)(2,1)S(1)} %bitcast.19), channel_id=1, replica_groups={{0,64,128,192,256,320,384,448},{8,72,136,200,264,328,392,456},{16,80,14..., dimensions={0} | all-to-all | bytes 557056 | tf_op jit(solution)/shard_map/all_to_all | solution.py:55
  85.2 0.4 shard_map.64
  85.6 11.1 %all_to_all.37 = bf16[4,8,2048]{2,1,0:T(8,128)(2,1)S(1)} all-to-all(bf16[4,8,2048]{2,1,0:T(8,128)(2,1)S(1)} %bitcast.22), channel_id=1, replica_groups={{0,128,256,384},{72,200,328,456},{16,144,272,400},{88,216,344,472},{32,..., dimensions={0} | all-to-all | bytes 262144 | tf_op jit(solution)/shard_map/all_to_all | solution.py:55
  96.7 1.1 broadcast_in_dim.26
  97.8 0.0 copy-start.3
  97.8 3.7 %all-to-all-start.5 = ((bf16[8,32,2048]{2,1,0:T(8,128)(2,1)}), bf16[8,32,2048]{2,1,0:T(8,128)(2,1)S(1)}, u32[]{:S(2)}, u32[]{:S(2)}) async-start(bf16[8,32,2048]{2,1,0:T(8,128)(2,1)} %broadcast_in_dim.26), calls=%async_computation.5 | async-start | bytes 2097152 | tf_op jit(solution)/shard_map/all_to_all | solution.py:55
  101.5 0.0 copy-done.3
  101.5 1.9 %collective-permute-start.2 = (bf16[2048,256]{1,0:T(8,128)(2,1)S(1)}, bf16[2048,256]{1,0:T(8,128)(2,1)S(1)}, u32[]{:S(2)}, u32[]{:S(2)}) collective-permute-start(bf16[2048,256]{1,0:T(8,128)(2,1)S(1)} %copy-done.3), channel_id=1, source_target_pairs={{0,8},{8,0},{16,24},{24,16},{32,40},{40,32},{48,56},{56,48},{64,72... | collective-permute-start | bytes 3145736 | tf_op jit(solution)/shard_map/ppermute | solution.py:409
  103.5 2.6 %collective-permute-done.2.w1_ref = bf16[2048,256]{1,0:T(8,128)(2,1)S(1)} collective-permute-done((bf16[2048,256]{1,0:T(8,128)(2,1)S(1)}, bf16[2048,256]{1,0:T(8,128)(2,1)S(1)}, u32[]{:S(2)}, u32[]{:S(2)}) %collective-permute-start.2) | collective-permute-done | bytes 1048608 | tf_op jit(solution)/shard_map/ppermute | solution.py:409
  106.1 5.9 %all-to-all-done.5.a_ref = bf16[8,32,2048]{2,1,0:T(8,128)(2,1)S(1)} async-done(((bf16[8,32,2048]{2,1,0:T(8,128)(2,1)}), bf16[8,32,2048]{2,1,0:T(8,128)(2,1)S(1)}, u32[]{:S(2)}, u32[]{:S(2)}) %all-to-all-start.5) | async-done | bytes 1048608 | tf_op jit(solution)/shard_map/all_to_all | solution.py:55
  112.0 0.7 shard_map.65
  112.8 20.3 %all_to_all.38 = bf16[16,32,256]{2,1,0:T(8,128)(2,1)S(1)} all-to-all(bf16[16,32,256]{2,1,0:T(8,128)(2,1)S(1)} %bitcast.21), channel_id=1, replica_groups={{0,1,2,3,4,5,6,7,8,9,10,11,12,13,14,15},{16,17,18,19,20,21,22,23,24,25,..., dimensions={0} | all-to-all | bytes 524288 | tf_op jit(solution)/shard_map/all_to_all | solution.py:55
  133.2 0.6 copy.8
  (6 shorter events, 0.1 us)
Async XLA Ops:
  0.0 29.3 %copy-start = (s32[8,4,64]{2,1,0:T(4,128)S(1)}, s32[8,4,64]{2,1,0:T(4,128)}, u32[]{:S(2)}) copy-start(s32[8,4,64]{2,1,0:T(4,128)} %param.10) | copy-start | bytes 24580
  1.5 22.2 %all-to-all-start = ((bf16[8,8,2048]{2,1,0:T(8,128)(2,1)}), bf16[8,8,2048]{2,1,0:T(8,128)(2,1)S(1)}, u32[]{:S(2)}, u32[]{:S(2)}) async-start(bf16[8,8,2048]{2,1,0:T(8,128)(2,1)} %broadcast_in_dim.10), calls=%async_computation | async-start | bytes 524288 | tf_op jit(solution)/shard_map/all_to_all | solution.py:55
  11.8 17.7 %collective-permute-start = (bf16[4096,128]{1,0:T(8,128)(2,1)}, bf16[4096,128]{1,0:T(8,128)(2,1)}, u32[]{:S(2)}, u32[]{:S(2)}) collective-permute-start(bf16[4096,128]{1,0:T(8,128)(2,1)} %rest_1_.3), channel_id=1, source_target_pairs={{0,8},{8,0},{16,24},{24,16},{32,40},{40,32},{48,56},{56,48},{64,72... | collective-permute-start | bytes 3145736 | tf_op jit(solution)/shard_map/ppermute | solution.py:400
  13.7 15.8 %collective-permute-start.1 = (bf16[4096,128]{1,0:T(8,128)(2,1)}, bf16[4096,128]{1,0:T(8,128)(2,1)}, u32[]{:S(2)}, u32[]{:S(2)}) collective-permute-start(bf16[4096,128]{1,0:T(8,128)(2,1)} %rest_2_.3), channel_id=1, source_target_pairs={{0,8},{8,0},{16,24},{24,16},{32,40},{40,32},{48,56},{56,48},{64,72... | collective-permute-start | bytes 3145736 | tf_op jit(solution)/shard_map/ppermute | solution.py:401
  24.8 4.8 %copy-start.1 = (bf16[4096,128]{1,0:T(8,128)(2,1)S(1)}, bf16[4096,128]{1,0:T(8,128)(2,1)}, u32[]{:S(2)}) copy-start(bf16[4096,128]{1,0:T(8,128)(2,1)} %rest_1_.3) | copy-start | bytes 3145732
  24.8 4.8 %copy-start.2 = (bf16[4096,128]{1,0:T(8,128)(2,1)S(1)}, bf16[4096,128]{1,0:T(8,128)(2,1)}, u32[]{:S(2)}) copy-start(bf16[4096,128]{1,0:T(8,128)(2,1)} %rest_2_.3) | copy-start | bytes 3145732
  24.8 17.7 %all-to-all-start.1 = ((bf16[4,64,2048]{2,1,0:T(8,128)(2,1)}), bf16[4,64,2048]{2,1,0:T(8,128)(2,1)S(1)}, u32[]{:S(2)}, u32[]{:S(2)}) async-start(bf16[4,64,2048]{2,1,0:T(8,128)(2,1)} %broadcast_in_dim.24), calls=%async_computation.1 | async-start | bytes 2097152 | tf_op jit(solution)/shard_map/all_to_all | solution.py:55
  35.9 0.7 copy-start.4
  50.6 17.3 %copy-start.5 = (bf16[64,2176]{1,0:T(8,128)(2,1)S(1)}, bf16[64,2176]{1,0:T(8,128)(2,1)}, u32[]{:S(2)}) copy-start(bf16[64,2176]{1,0:T(8,128)(2,1)} %copy-done.4) | copy-start | bytes 835588
  97.8 3.7 %copy-start.3 = (bf16[2048,256]{1,0:T(8,128)(2,1)S(1)}, bf16[2048,256]{1,0:T(8,128)(2,1)}, u32[]{:S(2)}) copy-start(bf16[2048,256]{1,0:T(8,128)(2,1)} %w0_ref) | copy-start | bytes 3145732
  97.8 14.2 %all-to-all-start.5 = ((bf16[8,32,2048]{2,1,0:T(8,128)(2,1)}), bf16[8,32,2048]{2,1,0:T(8,128)(2,1)S(1)}, u32[]{:S(2)}, u32[]{:S(2)}) async-start(bf16[8,32,2048]{2,1,0:T(8,128)(2,1)} %broadcast_in_dim.26), calls=%async_computation.5 | async-start | bytes 2097152 | tf_op jit(solution)/shard_map/all_to_all | solution.py:55
  101.5 4.6 %collective-permute-start.2 = (bf16[2048,256]{1,0:T(8,128)(2,1)S(1)}, bf16[2048,256]{1,0:T(8,128)(2,1)S(1)}, u32[]{:S(2)}, u32[]{:S(2)}) collective-permute-start(bf16[2048,256]{1,0:T(8,128)(2,1)S(1)} %copy-done.3), channel_id=1, source_target_pairs={{0,8},{8,0},{16,24},{24,16},{32,40},{40,32},{48,56},{56,48},{64,72... | collective-permute-start | bytes 3145736 | tf_op jit(solution)/shard_map/ppermute | solution.py:409

commit v4 on v3

--- a/solution.py
+++ b/solution.py
@@ -21,6 +21,8 @@
 STATE = WIDE + 128
 SCALE = math.log2(math.e) / math.sqrt(DH)
 NEG = -(2.0**100)
+REST_STEP = 4
+OWN_STEP = 4
 VMEM_LIMIT = 24 * 1024 * 1024
 F32 = jnp.float32
 BF16 = jnp.bfloat16
@@ -87,6 +89,8 @@
     top, total, acc, scaled, k_all, v_all, sems = rest[8 if alone else 6 :]
     local = k0_ref.shape[0]
     blocks = 2 * local // BLKSZ
+    found_at = NQB * blocks + 1
+    current_at = NQB * blocks + 2
     copies = []
     for i, (source, target, start) in enumerate(
         ((k0_ref, k_all, 0), (v0_ref, v_all, 0), (k1_ref, k_all, local), (v1_ref, v_all, local))
@@ -97,124 +101,100 @@
 
     if alone:
 
-        def collect(c, carry):
-            listed[c, blocks + 1] = -1
-
-            def look(b, found):
-                kind = hits_ref[c, b]
-                listed[c, found] = b
-
-                @pl.when(kind == 2)
-                def _():
-                    listed[c, blocks + 1] = b
-
-                return found + jnp.where(kind == 1, 1, 0)
-
-            listed[c, blocks] = lax.fori_loop(0, blocks, look, 0)
-            return carry
-
-        lax.fori_loop(0, NQB, collect, 0)
+        def collect(at, found):
+            kind = hits_ref[at // blocks, at % blocks]
+            listed[found] = at
+
+            @pl.when(kind == 2)
+            def _():
+                listed[current_at] = at % blocks
+
+            return found + jnp.where(kind == 1, 1, 0)
+
+        listed[current_at] = -1
+        listed[found_at] = lax.fori_loop(0, NQB * blocks, collect, 0)
 
     def block_of(ref, b):
         return ref[pl.ds(pl.multiple_of(b * BLKSZ, BLKSZ), BLKSZ), :]
 
-    def rows_of(i):
-        return slice(i * tile, (i + 1) * tile)
-
-    def score(i, group):
-        kblk = jnp.concatenate([block_of(k_all, b) for b in group], axis=0)
+    def state_of(ref, c, i):
+        return ref.at[c, i * tile : (i + 1) * tile]
+
+    def score(c, i, b):
+        kblk = block_of(k_all, b)
         return lax.dot_general(
-            scaled[rows_of(i)],
+            state_of(scaled, c, i)[...],
             jnp.concatenate([kblk, kblk], axis=1),
             (((1,), (1,)), ((), ())),
             preferred_element_type=F32,
         )
 
-    def soften(i, scores):
-        old_top = top[rows_of(i)]
+    def soften(c, i, scores):
+        top_ref, total_ref = state_of(top, c, i), state_of(total, c, i)
+        old_top = top_ref[...]
         new_top = jnp.maximum(old_top, jnp.max(scores, axis=1, keepdims=True))
         fade = jnp.exp2(old_top - new_top)
         probs = []
         added = None
-        for j in range(scores.shape[1] // 128):
+        for j in range(BLKSZ // 128):
             part = jnp.exp2(scores[:, j * 128 : (j + 1) * 128] - new_top)
             added = part if added is None else added + part
             probs.append(part.astype(BF16))
-        top[rows_of(i)] = new_top
-        total[rows_of(i)] = total[rows_of(i)] * fade + added
+        top_ref[...] = new_top
+        total_ref[...] = total_ref[...] * fade + added
         return jnp.concatenate(probs, axis=1), fade
 
-    def gather(i, group, probs, fade):
-        vblk = jnp.concatenate([block_of(v_all, b) for b in group], axis=0)
-        acc[rows_of(i)] = acc[rows_of(i)] * fade + jnp.dot(probs, vblk, preferred_element_type=F32)
-
-    def run(work, mask=None):
+    def gather(c, i, b, probs, fade):
+        acc_ref = state_of(acc, c, i)
+        acc_ref[...] = acc_ref[...] * fade + jnp.dot(
+            probs, block_of(v_all, b), preferred_element_type=F32
+        )
+
+    def run(items, masked=False):
+        work = [(c, i, b) for c, b in items for i in range(len(parts))]
         scores = score(*work[0])
         before = None
-        for at, (i, group) in enumerate(work):
+        for at, (c, i, b) in enumerate(work):
             following = score(*work[at + 1]) if at + 1 < len(work) else None
-            if mask is not None:
-                scores = jnp.where(mask(i), scores, NEG)
-            probs, fade = soften(i, scores)
+            if masked:
+                row = lax.broadcasted_iota(jnp.int32, (tile, BLKSZ), 0) % 16
+                token = (((2 * c + row // 8) * XN + parts[i]) * 2 + core) * ROWS + row % 8
+                position = lax.broadcasted_iota(jnp.int32, (tile, BLKSZ), 1)
+                scores = jnp.where(position <= token, scores, NEG)
+            probs, fade = soften(c, i, scores)
             if before is not None:
                 gather(*before)
-            before = (i, group, probs, fade)
+            before = (c, i, b, probs, fade)
             scores = following
         gather(*before)
 
-    def prepare(c):
-        top[...] = jnp.full(top.shape, NEG, F32)
-        total[...] = jnp.zeros(total.shape, F32)
-        acc[...] = jnp.zeros(acc.shape, F32)
+    def prepare(c, carry):
         for i, x in enumerate(parts):
             source = q_ref.at[c] if alone else q_ref.at[x, c]
             rows = jnp.concatenate([source[:, h * DH : (h + 1) * DH] for h in range(GROUP)], axis=0)
             rows = rows.astype(F32) * SCALE
             high = rows.astype(BF16)
             low = (rows - high.astype(F32)).astype(BF16)
-            scaled[rows_of(i)] = jnp.concatenate([high, low], axis=1)
+            state_of(scaled, c, i)[...] = jnp.concatenate([high, low], axis=1)
+        return carry
+
+    def item(at):
+        return listed[at] // blocks, listed[at] % blocks
+
+    def several(j, carry):
+        run([item(step * j + at) for at in range(step)])
+        return carry
 
     def query_block(c, carry):
-        @pl.when(c > 0)
-        def _():
-            prepare(c)
-
-        found = listed[c, blocks]
-        current = listed[c, blocks + 1]
-        span = range(len(parts))
-
-        def two(j, carry):
-            first, second = listed[c, 2 * j], listed[c, 2 * j + 1]
-            if alone:
-                run([(i, [b]) for b in (first, second) for i in span])
-            else:
-                run([(i, [first, second]) for i in span])
-            return carry
-
-        lax.fori_loop(0, found // 2, two, 0)
-
-        @pl.when(found % 2 == 1)
-        def _():
-            run([(i, [listed[c, found - 1]]) for i in span])
-
-        @pl.when(current >= 0)
-        def _():
-            def mask(i):
-                row = lax.broadcasted_iota(jnp.int32, (tile, BLKSZ), 0) % 16
-                token = (((2 * c + row // 8) * XN + parts[i]) * 2 + core) * ROWS + row % 8
-                return lax.broadcasted_iota(jnp.int32, (tile, BLKSZ), 1) <= token
-
-            run([(i, [current]) for i in span], mask)
-
         first = pl.multiple_of(c * 16, 16)
         lane = lax.broadcasted_iota(jnp.int32, (16, 128), 1)
         for i, x in enumerate(parts):
             target = out_ref if alone else out_ref.at[x]
-            peak = top[rows_of(i)]
+            peak = state_of(top, c, i)[...]
             kept = peak.astype(BF16).astype(F32)
             factor = jnp.exp2(peak - kept)
-            values = (acc[rows_of(i)] * factor).astype(BF16)
-            summed = jnp.sum(total[rows_of(i)], axis=1, keepdims=True) * factor
+            values = (state_of(acc, c, i)[...] * factor).astype(BF16)
+            summed = jnp.sum(state_of(total, c, i)[...], axis=1, keepdims=True) * factor
             high = summed.astype(BF16).astype(F32)
             low = summed - high
             stats = jnp.zeros((16, 128), F32)
@@ -227,9 +207,30 @@
             target[pl.ds(first, 16), WIDE:] = stats.astype(BF16)
         return carry
 
-    prepare(0)
+    top[...] = jnp.full(top.shape, NEG, F32)
+    total[...] = jnp.zeros(total.shape, F32)
+    acc[...] = jnp.zeros(acc.shape, F32)
+    lax.fori_loop(0, NQB, prepare, 0)
     for copy in copies:
         copy.wait()
+    found = listed[found_at]
+    current = listed[current_at]
+    step = OWN_STEP if alone else REST_STEP
+    lax.fori_loop(0, found // step, several, 0)
+    rest_at = found // step * step
+
+    @pl.when(found - rest_at >= 2)
+    def _():
+        run([item(rest_at), item(rest_at + 1)])
+
+    @pl.when((found - rest_at) % 2 == 1)
+    def _():
+        run([item(found - 1)])
+
+    @pl.when(current >= 0)
+    def _():
+        run([(c, current) for c in range(NQB)], masked=True)
+
     lax.fori_loop(0, NQB, query_block, 0)
     if alone:
         copy = pltpu.make_async_copy(out_ref, final_ref, sems.at[4])
@@ -240,10 +241,10 @@
 def state_scratch(parts, tokens):
     tile = parts * GROUP * 16
     return [
-        pltpu.VMEM((tile, 128), F32),
-        pltpu.VMEM((tile, 128), F32),
-        pltpu.VMEM((tile, DH), F32),
-        pltpu.VMEM((tile, 2 * DH), BF16),
+        pltpu.VMEM((NQB, tile, 128), F32),
+        pltpu.VMEM((NQB, tile, 128), F32),
+        pltpu.VMEM((NQB, tile, DH), F32),
+        pltpu.VMEM((NQB, tile, 2 * DH), BF16),
         pltpu.VMEM((tokens, DH), BF16),
         pltpu.VMEM((tokens, DH), BF16),
         pltpu.SemaphoreType.DMA((5,)),
@@ -261,7 +262,7 @@
     return pl.pallas_call(
         functools.partial(attend_kernel, True),
         name="attend_own",
-        out_shape=(state, jax.ShapeDtypeStruct((NQB, tokens // BLKSZ + 8), jnp.int32)),
+        out_shape=(state, jax.ShapeDtypeStruct((NQB * tokens // BLKSZ + 8,), jnp.int32)),
         in_specs=[in_smem(), in_vmem(), in_smem()] + [in_hbm()] * 4,
         out_specs=(in_hbm(), in_smem()),
         scratch_shapes=[pltpu.VMEM(state.shape, BF16)] + state_scratch(1, tokens),

time: 135 us -> 132 us (0.978)
  Pallas kernels: 16.7 us -> 13.2 us
  waiting for transfers between devices: 21 us -> 22.5 us
    pallas_call x1, Pallas kernels: 8.07 us -> 5.98 us  [attend_rest(): pl.pallas_call(functools.partial(attend_kernel, False), name='attend_rest...]
    pallas_call x1, Pallas kernels: 6.31 us -> 4.82 us  [attend_own(): pl.pallas_call(functools.partial(attend_kernel, True), name='attend_own',...]
    all_to_all x3, waiting for transfers between devices: 18.4 us -> 19.9 us  [exchange(): lax.all_to_all(blocks, axis, split_axis=0, concat_axis=0, tiled=True, axi...]
  transfers between devices with their start and end apart: 6 -> 6, of which waited for: 4 -> 4; matrix products, arithmetic and copies ran while one was open for 2% -> 2% of each run, Pallas kernels for 5% -> 4%
where the time goes in v4:
time: 132 us
  blocking collectives  64.8 us (49%)
  starting transfers between devices  24.7 us (19%)
  waiting for transfers between devices  22.5 us (17%)
  Pallas kernels  13.2 us (10%)
  local copies, waits for them, and re-layouts  6.01 us (5%)
    all_to_all x4, blocking collectives, exchange(): lax.all_to_all(blocks, axis, split_axis=0, concat_axis=0, tiled=True, axi...  64.8 us
    all_to_all x3, waiting for transfers between devices, exchange(): lax.all_to_all(blocks, axis, split_axis=0, concat_axis=0, tiled=True, axi...  19.9 us
    all_to_all x3, starting transfers between devices, exchange(): lax.all_to_all(blocks, axis, split_axis=0, concat_axis=0, tiled=True, axi...  18.4 us
    pallas_call x1, Pallas kernels, attend_rest(): pl.pallas_call(functools.partial(attend_kernel, False), name='attend_rest...  5.98 us
    pallas_call x1, Pallas kernels, attend_own(): pl.pallas_call(functools.partial(attend_kernel, True), name='attend_own',...  4.82 us
    broadcast_in_dim x3, local copies, waits for them, and re-layouts, spread(): jnp.broadcast_to(rows[None], (count,) + rows.shape)  3.69 us
  transfers between devices with their start and end apart: 6, of which 4 were waited for; matrix products, arithmetic and copies ran while one was open for 2% of the time, Pallas kernels for 4%

profile of v4, /device:TPU:8, one launch (start us, length us, event | category | flops | bytes accessed | tf_op | source)
XLA Modules:
  0.0 131.7 jit_solution(7935142204168759097)
XLA Ops:
  0.0 0.0 copy-start
  0.0 1.5 %broadcast_in_dim.10 = bf16[8,8,2048]{2,1,0:T(8,128)(2,1)} broadcast(bf16[8,2048]{1,0:T(8,128)(2,1)} %param.6), dimensions={1,2} | broadcast | bytes 294912 | tf_op jit(solution)/shard_map/broadcast_in_dim | solution.py:64
  1.5 10.3 %all-to-all-start = ((bf16[8,8,2048]{2,1,0:T(8,128)(2,1)}), bf16[8,8,2048]{2,1,0:T(8,128)(2,1)S(1)}, u32[]{:S(2)}, u32[]{:S(2)}) async-start(bf16[8,8,2048]{2,1,0:T(8,128)(2,1)} %broadcast_in_dim.10), calls=%async_computation | async-start | bytes 524288 | tf_op jit(solution)/shard_map/all_to_all | solution.py:57
  11.8 1.9 %collective-permute-start = (bf16[4096,128]{1,0:T(8,128)(2,1)}, bf16[4096,128]{1,0:T(8,128)(2,1)}, u32[]{:S(2)}, u32[]{:S(2)}) collective-permute-start(bf16[4096,128]{1,0:T(8,128)(2,1)} %rest_1_.3), channel_id=1, source_target_pairs={{0,8},{8,0},{16,24},{24,16},{32,40},{40,32},{48,56},{56,48},{64,72... | collective-permute-start | bytes 3145736 | tf_op jit(solution)/shard_map/ppermute | solution.py:401
  13.7 2.4 %collective-permute-start.1 = (bf16[4096,128]{1,0:T(8,128)(2,1)}, bf16[4096,128]{1,0:T(8,128)(2,1)}, u32[]{:S(2)}, u32[]{:S(2)}) collective-permute-start(bf16[4096,128]{1,0:T(8,128)(2,1)} %rest_2_.3), channel_id=1, source_target_pairs={{0,8},{8,0},{16,24},{24,16},{32,40},{40,32},{48,56},{56,48},{64,72... | collective-permute-start | bytes 3145736 | tf_op jit(solution)/shard_map/ppermute | solution.py:402
  16.2 0.8 dynamic_slice.8
  16.9 0.1 reshape.43
  17.1 0.1 eq.35
  17.1 6.5 %all-to-all-done = bf16[8,8,2048]{2,1,0:T(8,128)(2,1)S(1)} async-done(((bf16[8,8,2048]{2,1,0:T(8,128)(2,1)}), bf16[8,8,2048]{2,1,0:T(8,128)(2,1)S(1)}, u32[]{:S(2)}, u32[]{:S(2)}) %all-to-all-start) | async-done | bytes 262176 | tf_op jit(solution)/shard_map/all_to_all | solution.py:57
  23.7 1.1 broadcast_in_dim.24
  24.8 0.0 copy-start.1
  24.8 0.0 copy-start.2
  24.8 4.4 %all-to-all-start.1 = ((bf16[4,64,2048]{2,1,0:T(8,128)(2,1)}), bf16[4,64,2048]{2,1,0:T(8,128)(2,1)S(1)}, u32[]{:S(2)}, u32[]{:S(2)}) async-start(bf16[4,64,2048]{2,1,0:T(8,128)(2,1)} %broadcast_in_dim.24), calls=%async_computation.1 | async-start | bytes 2097152 | tf_op jit(solution)/shard_map/all_to_all | solution.py:57
  29.2 0.1 pad_add_fusion.place_ref
  29.3 0.0 copy-done
  29.3 0.2 compare_reduce_fusion
  29.5 0.0 collective-permute-done.rest_3_
  29.6 0.0 collective-permute-done.1.rest_4_
  29.6 0.0 copy-done.1
  29.6 0.0 copy-done.2
  29.6 4.8 %attend_own.1 = (bf16[64,2176]{1,0:T(8,128)(2,1)S(1)}, s32[72]{0:T(128)S(1)}) custom-call(s32[2]{0:T(128)S(1)} %pad_add_fusion.place_ref, bf16[4,16,2048]{2,1,0:T(8,128)(2,1)S(1)} %bitcast.18, s32[4,16]{1,0:T(4,128)S(1)} %broadcast_select_fusion.rest_0_, bf16[4096,128]{1,0:T(8,128)(2,1)S(1)} %copy-done.1, bf16[4096,128]{1,0:T(8,128)(2,1)S(1)} %copy-done.2, ...), custom_call_target="tpu_custom_call" | custom-call | flops 536870912 | bytes 8388608 | tf_op jit(solution)/shard_map/attend_own/pallas_call | solution.py:262
  34.4 0.0 copy-start.4
  34.4 0.7 copy-done.4
  35.1 7.4 %all-to-all-done.1 = bf16[4,64,2048]{2,1,0:T(8,128)(2,1)S(1)} async-done(((bf16[4,64,2048]{2,1,0:T(8,128)(2,1)}), bf16[4,64,2048]{2,1,0:T(8,128)(2,1)S(1)}, u32[]{:S(2)}, u32[]{:S(2)}) %all-to-all-start.1) | async-done | bytes 1048608 | tf_op jit(solution)/shard_map/all_to_all | solution.py:57
  42.5 6.0 %attend_rest.1 = bf16[4,64,2176]{2,1,0:T(8,128)(2,1)S(1)} custom-call(s32[2]{0:T(128)S(1)} %pad_add_fusion.place_ref, bf16[4,4,16,2048]{3,2,1,0:T(8,128)(2,1)S(1)} %bitcast.16, s32[72]{0:T(128)S(1)} %get-tuple-element.10.rest_0_, bf16[4096,128]{1,0:T(8,128)(2,1)S(1)} %copy-done.1, bf16[4096,128]{1,0:T(8,128)(2,1)S(1)} %copy-done.2, ...), custom_call_target="tpu_custom_call" | custom-call | flops 1610612736 | bytes 8388608 | tf_op jit(solution)/shard_map/attend_rest/pallas_call | solution.py:275
  48.5 0.0 copy-start.5
  48.5 16.9 %all_to_all.35.in_ref = bf16[4,64,2176]{2,1,0:T(8,128)(2,1)S(1)} all-to-all(bf16[4,64,2176]{2,1,0:T(8,128)(2,1)S(1)} %attend_rest.1), channel_id=1, replica_groups={{0,16,32,48},{8,24,40,56},{64,80,96,112},{72,88,104,120},{128,144,160,1..., dimensions={0} | all-to-all | bytes 2228224 | tf_op jit(solution)/shard_map/all_to_all | solution.py:57
  65.4 0.0 copy-done.5
  65.4 1.3 merge.1
  66.7 17.7 %all_to_all.36 = bf16[8,8,2176]{2,1,0:T(8,128)(2,1)S(1)} all-to-all(bf16[8,8,2176]{2,1,0:T(8,128)(2,1)S(1)} %bitcast.19), channel_id=1, replica_groups={{0,64,128,192,256,320,384,448},{8,72,136,200,264,328,392,456},{16,80,14..., dimensions={0} | all-to-all | bytes 557056 | tf_op jit(solution)/shard_map/all_to_all | solution.py:57
  84.4 0.4 shard_map.64
  84.8 11.1 %all_to_all.37 = bf16[4,8,2048]{2,1,0:T(8,128)(2,1)S(1)} all-to-all(bf16[4,8,2048]{2,1,0:T(8,128)(2,1)S(1)} %bitcast.22), channel_id=1, replica_groups={{0,128,256,384},{72,200,328,456},{16,144,272,400},{88,216,344,472},{32,..., dimensions={0} | all-to-all | bytes 262144 | tf_op jit(solution)/shard_map/all_to_all | solution.py:57
  95.9 1.1 broadcast_in_dim.26
  97.0 0.0 copy-start.3
  97.0 3.7 %all-to-all-start.5 = ((bf16[8,32,2048]{2,1,0:T(8,128)(2,1)}), bf16[8,32,2048]{2,1,0:T(8,128)(2,1)S(1)}, u32[]{:S(2)}, u32[]{:S(2)}) async-start(bf16[8,32,2048]{2,1,0:T(8,128)(2,1)} %broadcast_in_dim.26), calls=%async_computation.5 | async-start | bytes 2097152 | tf_op jit(solution)/shard_map/all_to_all | solution.py:57
  100.7 0.0 copy-done.3
  100.7 1.9 %collective-permute-start.2 = (bf16[2048,256]{1,0:T(8,128)(2,1)S(1)}, bf16[2048,256]{1,0:T(8,128)(2,1)S(1)}, u32[]{:S(2)}, u32[]{:S(2)}) collective-permute-start(bf16[2048,256]{1,0:T(8,128)(2,1)S(1)} %copy-done.3), channel_id=1, source_target_pairs={{0,8},{8,0},{16,24},{24,16},{32,40},{40,32},{48,56},{56,48},{64,72... | collective-permute-start | bytes 3145736 | tf_op jit(solution)/shard_map/ppermute | solution.py:410
  102.7 2.6 %collective-permute-done.2.w1_ref = bf16[2048,256]{1,0:T(8,128)(2,1)S(1)} collective-permute-done((bf16[2048,256]{1,0:T(8,128)(2,1)S(1)}, bf16[2048,256]{1,0:T(8,128)(2,1)S(1)}, u32[]{:S(2)}, u32[]{:S(2)}) %collective-permute-start.2) | collective-permute-done | bytes 1048608 | tf_op jit(solution)/shard_map/ppermute | solution.py:410
  105.3 5.9 %all-to-all-done.5.a_ref = bf16[8,32,2048]{2,1,0:T(8,128)(2,1)S(1)} async-done(((bf16[8,32,2048]{2,1,0:T(8,128)(2,1)}), bf16[8,32,2048]{2,1,0:T(8,128)(2,1)S(1)}, u32[]{:S(2)}, u32[]{:S(2)}) %all-to-all-start.5) | async-done | bytes 1048608 | tf_op jit(solution)/shard_map/all_to_all | solution.py:57
  111.2 0.7 shard_map.65
  112.0 19.0 %all_to_all.38 = bf16[16,32,256]{2,1,0:T(8,128)(2,1)S(1)} all-to-all(bf16[16,32,256]{2,1,0:T(8,128)(2,1)S(1)} %bitcast.21), channel_id=1, replica_groups={{0,1,2,3,4,5,6,7,8,9,10,11,12,13,14,15},{16,17,18,19,20,21,22,23,24,25,..., dimensions={0} | all-to-all | bytes 524288 | tf_op jit(solution)/shard_map/all_to_all | solution.py:57
  131.0 0.6 copy.8
  (6 shorter events, 0.1 us)
Async XLA Ops:
  0.0 29.3 %copy-start = (s32[8,4,64]{2,1,0:T(4,128)S(1)}, s32[8,4,64]{2,1,0:T(4,128)}, u32[]{:S(2)}) copy-start(s32[8,4,64]{2,1,0:T(4,128)} %param.10) | copy-start | bytes 24580
  1.5 22.2 %all-to-all-start = ((bf16[8,8,2048]{2,1,0:T(8,128)(2,1)}), bf16[8,8,2048]{2,1,0:T(8,128)(2,1)S(1)}, u32[]{:S(2)}, u32[]{:S(2)}) async-start(bf16[8,8,2048]{2,1,0:T(8,128)(2,1)} %broadcast_in_dim.10), calls=%async_computation | async-start | bytes 524288 | tf_op jit(solution)/shard_map/all_to_all | solution.py:57
  11.8 17.7 %collective-permute-start = (bf16[4096,128]{1,0:T(8,128)(2,1)}, bf16[4096,128]{1,0:T(8,128)(2,1)}, u32[]{:S(2)}, u32[]{:S(2)}) collective-permute-start(bf16[4096,128]{1,0:T(8,128)(2,1)} %rest_1_.3), channel_id=1, source_target_pairs={{0,8},{8,0},{16,24},{24,16},{32,40},{40,32},{48,56},{56,48},{64,72... | collective-permute-start | bytes 3145736 | tf_op jit(solution)/shard_map/ppermute | solution.py:401
  13.7 15.8 %collective-permute-start.1 = (bf16[4096,128]{1,0:T(8,128)(2,1)}, bf16[4096,128]{1,0:T(8,128)(2,1)}, u32[]{:S(2)}, u32[]{:S(2)}) collective-permute-start(bf16[4096,128]{1,0:T(8,128)(2,1)} %rest_2_.3), channel_id=1, source_target_pairs={{0,8},{8,0},{16,24},{24,16},{32,40},{40,32},{48,56},{56,48},{64,72... | collective-permute-start | bytes 3145736 | tf_op jit(solution)/shard_map/ppermute | solution.py:402
  24.8 4.8 %copy-start.1 = (bf16[4096,128]{1,0:T(8,128)(2,1)S(1)}, bf16[4096,128]{1,0:T(8,128)(2,1)}, u32[]{:S(2)}) copy-start(bf16[4096,128]{1,0:T(8,128)(2,1)} %rest_1_.3) | copy-start | bytes 3145732
  24.8 4.8 %copy-start.2 = (bf16[4096,128]{1,0:T(8,128)(2,1)S(1)}, bf16[4096,128]{1,0:T(8,128)(2,1)}, u32[]{:S(2)}) copy-start(bf16[4096,128]{1,0:T(8,128)(2,1)} %rest_2_.3) | copy-start | bytes 3145732
  24.8 17.7 %all-to-all-start.1 = ((bf16[4,64,2048]{2,1,0:T(8,128)(2,1)}), bf16[4,64,2048]{2,1,0:T(8,128)(2,1)S(1)}, u32[]{:S(2)}, u32[]{:S(2)}) async-start(bf16[4,64,2048]{2,1,0:T(8,128)(2,1)} %broadcast_in_dim.24), calls=%async_computation.1 | async-start | bytes 2097152 | tf_op jit(solution)/shard_map/all_to_all | solution.py:57
  34.4 0.7 copy-start.4
  48.5 16.9 %copy-start.5 = (bf16[64,2176]{1,0:T(8,128)(2,1)S(1)}, bf16[64,2176]{1,0:T(8,128)(2,1)}, u32[]{:S(2)}) copy-start(bf16[64,2176]{1,0:T(8,128)(2,1)} %copy-done.4) | copy-start | bytes 835588
  97.0 3.7 %copy-start.3 = (bf16[2048,256]{1,0:T(8,128)(2,1)S(1)}, bf16[2048,256]{1,0:T(8,128)(2,1)}, u32[]{:S(2)}) copy-start(bf16[2048,256]{1,0:T(8,128)(2,1)} %w0_ref) | copy-start | bytes 3145732
  97.0 14.2 %all-to-all-start.5 = ((bf16[8,32,2048]{2,1,0:T(8,128)(2,1)}), bf16[8,32,2048]{2,1,0:T(8,128)(2,1)S(1)}, u32[]{:S(2)}, u32[]{:S(2)}) async-start(bf16[8,32,2048]{2,1,0:T(8,128)(2,1)} %broadcast_in_dim.26), calls=%async_computation.5 | async-start | bytes 2097152 | tf_op jit(solution)/shard_map/all_to_all | solution.py:57
  100.7 4.6 %collective-permute-start.2 = (bf16[2048,256]{1,0:T(8,128)(2,1)S(1)}, bf16[2048,256]{1,0:T(8,128)(2,1)S(1)}, u32[]{:S(2)}, u32[]{:S(2)}) collective-permute-start(bf16[2048,256]{1,0:T(8,128)(2,1)S(1)} %copy-done.3), channel_id=1, source_target_pairs={{0,8},{8,0},{16,24},{24,16},{32,40},{40,32},{48,56},{56,48},{64,72... | collective-permute-start | bytes 3145736 | tf_op jit(solution)/shard_map/ppermute | solution.py:410

commit v5 on v4

--- a/solution.py
+++ b/solution.py
@@ -84,9 +84,9 @@
         hits_ref, k0_ref, v0_ref, k1_ref, v1_ref, final_ref, listed, out_ref = rest[:8]
         parts = [column]
     else:
-        listed, k0_ref, v0_ref, k1_ref, v1_ref, out_ref = rest[:6]
+        listed, k0_ref, v0_ref, k1_ref, v1_ref, final_ref, out_ref = rest[:7]
         parts = [lax.rem(column + j, XN) for j in range(1, XN)]
-    top, total, acc, scaled, k_all, v_all, sems = rest[8 if alone else 6 :]
+    top, total, acc, scaled, k_all, v_all, sems = rest[8 if alone else 7 :]
     local = k0_ref.shape[0]
     blocks = 2 * local // BLKSZ
     found_at = NQB * blocks + 1
@@ -184,6 +184,12 @@
     def several(j, carry):
         run([item(step * j + at) for at in range(step)])
         return carry
+
+    def leave(c, i):
+        rows = pl.ds(pl.multiple_of(c * 16, 16), 16)
+        return pltpu.make_async_copy(
+            out_ref.at[parts[i], rows], final_ref.at[parts[i], rows], sems.at[4 + c * len(parts) + i]
+        )
 
     def query_block(c, carry):
         first = pl.multiple_of(c * 16, 16)
@@ -205,6 +211,8 @@
                 stats = jnp.where(lane == GROUP + h, high[rows], stats)
                 stats = jnp.where(lane == 2 * GROUP + h, low[rows], stats)
             target[pl.ds(first, 16), WIDE:] = stats.astype(BF16)
+            if not alone:
+                leave(c, i).start()
         return carry
 
     top[...] = jnp.full(top.shape, NEG, F32)
@@ -232,6 +240,10 @@
         run([(c, current) for c in range(NQB)], masked=True)
 
     lax.fori_loop(0, NQB, query_block, 0)
+    if not alone:
+        for c in range(NQB):
+            for i in range(len(parts)):
+                leave(c, i).wait()
     if alone:
         copy = pltpu.make_async_copy(out_ref, final_ref, sems.at[4])
         copy.start()
@@ -247,7 +259,7 @@
         pltpu.VMEM((NQB, tile, 2 * DH), BF16),
         pltpu.VMEM((tokens, DH), BF16),
         pltpu.VMEM((tokens, DH), BF16),
-        pltpu.SemaphoreType.DMA((5,)),
+        pltpu.SemaphoreType.DMA((4 + NQB * parts,)),
     ]
 
 
@@ -272,13 +284,14 @@
 
 
 def attend_rest(where, q, listed, cache):
+    states = jax.ShapeDtypeStruct((XN, NQB * 16, STATE), BF16)
     return pl.pallas_call(
         functools.partial(attend_kernel, False),
         name="attend_rest",
-        out_shape=jax.ShapeDtypeStruct((XN, NQB * 16, STATE), BF16),
+        out_shape=states,
         in_specs=[in_smem(), in_vmem(), in_smem()] + [in_hbm()] * 4,
-        out_specs=in_vmem(),
-        scratch_shapes=state_scratch(XN - 1, 2 * cache[0].shape[0]),
+        out_specs=in_hbm(),
+        scratch_shapes=[pltpu.VMEM(states.shape, BF16)] + state_scratch(XN - 1, 2 * cache[0].shape[0]),
         compiler_params=pltpu.CompilerParams(vmem_limit_bytes=VMEM_LIMIT),
         cost_estimate=attend_cost(XN - 1),
     )(where, q, listed, *cache)

time: 132 us -> 133 us (level)
  Pallas kernels: 13.2 us -> 16.7 us
  blocking collectives: 64.8 us -> 62.2 us
    pallas_call x1, Pallas kernels: 5.98 us -> 9.09 us  [attend_rest(): pl.pallas_call(functools.partial(attend_kernel, False), name='attend_rest...]
    all_to_all x4, blocking collectives: 64.8 us -> 62.2 us  [exchange(): lax.all_to_all(blocks, axis, split_axis=0, concat_axis=0, tiled=True, axi...]
where the time goes in v5:
time: 133 us; the launch traced here: 132 us
  blocking collectives  62.2 us (47%)
  starting transfers between devices  24.7 us (19%)
  waiting for transfers between devices  22.1 us (17%)
  Pallas kernels  16.7 us (13%)
  local copies, waits for them, and re-layouts  6.01 us (5%)
    all_to_all x4, blocking collectives, exchange(): lax.all_to_all(blocks, axis, split_axis=0, concat_axis=0, tiled=True, axi...  62.2 us
    all_to_all x3, waiting for transfers between devices, exchange(): lax.all_to_all(blocks, axis, split_axis=0, concat_axis=0, tiled=True, axi...  19.4 us
    all_to_all x3, starting transfers between devices, exchange(): lax.all_to_all(blocks, axis, split_axis=0, concat_axis=0, tiled=True, axi...  18.4 us
    pallas_call x1, Pallas kernels, attend_rest(): pl.pallas_call(functools.partial(attend_kernel, False), name='attend_rest...  9.09 us
    pallas_call x1, Pallas kernels, attend_own(): pl.pallas_call(functools.partial(attend_kernel, True), name='attend_own',...  5.26 us
    broadcast_in_dim x3, local copies, waits for them, and re-layouts, spread(): jnp.broadcast_to(rows[None], (count,) + rows.shape)  3.69 us
  transfers between devices with their start and end apart: 6, of which 4 were waited for; matrix products, arithmetic and copies ran while one was open for 2% of the time, Pallas kernels for 4%

profile of v5, /device:TPU:8, one launch (start us, length us, event | category | flops | bytes accessed | tf_op | source)
XLA Modules:
  0.0 132.2 jit_solution(7016370773155393913)
XLA Ops:
  0.0 0.0 copy-start
  0.0 1.5 %broadcast_in_dim.10 = bf16[8,8,2048]{2,1,0:T(8,128)(2,1)} broadcast(bf16[8,2048]{1,0:T(8,128)(2,1)} %param.6), dimensions={1,2} | broadcast | bytes 294912 | tf_op jit(solution)/shard_map/broadcast_in_dim | solution.py:64
  1.5 10.3 %all-to-all-start = ((bf16[8,8,2048]{2,1,0:T(8,128)(2,1)}), bf16[8,8,2048]{2,1,0:T(8,128)(2,1)S(1)}, u32[]{:S(2)}, u32[]{:S(2)}) async-start(bf16[8,8,2048]{2,1,0:T(8,128)(2,1)} %broadcast_in_dim.10), calls=%async_computation | async-start | bytes 524288 | tf_op jit(solution)/shard_map/all_to_all | solution.py:57
  11.8 1.9 %collective-permute-start = (bf16[4096,128]{1,0:T(8,128)(2,1)}, bf16[4096,128]{1,0:T(8,128)(2,1)}, u32[]{:S(2)}, u32[]{:S(2)}) collective-permute-start(bf16[4096,128]{1,0:T(8,128)(2,1)} %rest_1_.3), channel_id=1, source_target_pairs={{0,8},{8,0},{16,24},{24,16},{32,40},{40,32},{48,56},{56,48},{64,72... | collective-permute-start | bytes 3145736 | tf_op jit(solution)/shard_map/ppermute | solution.py:414
  13.7 2.4 %collective-permute-start.1 = (bf16[4096,128]{1,0:T(8,128)(2,1)}, bf16[4096,128]{1,0:T(8,128)(2,1)}, u32[]{:S(2)}, u32[]{:S(2)}) collective-permute-start(bf16[4096,128]{1,0:T(8,128)(2,1)} %rest_2_.3), channel_id=1, source_target_pairs={{0,8},{8,0},{16,24},{24,16},{32,40},{40,32},{48,56},{56,48},{64,72... | collective-permute-start | bytes 3145736 | tf_op jit(solution)/shard_map/ppermute | solution.py:415
  16.2 0.8 dynamic_slice.8
  16.9 0.1 reshape.43
  17.1 0.1 eq.35
  17.1 6.5 %all-to-all-done = bf16[8,8,2048]{2,1,0:T(8,128)(2,1)S(1)} async-done(((bf16[8,8,2048]{2,1,0:T(8,128)(2,1)}), bf16[8,8,2048]{2,1,0:T(8,128)(2,1)S(1)}, u32[]{:S(2)}, u32[]{:S(2)}) %all-to-all-start) | async-done | bytes 262176 | tf_op jit(solution)/shard_map/all_to_all | solution.py:57
  23.7 1.1 broadcast_in_dim.24
  24.8 0.0 copy-start.1
  24.8 0.0 copy-start.2
  24.8 4.4 %all-to-all-start.1 = ((bf16[4,64,2048]{2,1,0:T(8,128)(2,1)}), bf16[4,64,2048]{2,1,0:T(8,128)(2,1)S(1)}, u32[]{:S(2)}, u32[]{:S(2)}) async-start(bf16[4,64,2048]{2,1,0:T(8,128)(2,1)} %broadcast_in_dim.24), calls=%async_computation.1 | async-start | bytes 2097152 | tf_op jit(solution)/shard_map/all_to_all | solution.py:57
  29.2 0.1 pad_add_fusion.place_ref
  29.3 0.0 copy-done
  29.3 0.2 compare_reduce_fusion
  29.5 0.0 collective-permute-done.rest_3_
  29.6 0.0 collective-permute-done.1.rest_4_
  29.6 0.0 copy-done.1
  29.6 0.0 copy-done.2
  29.6 5.3 %attend_own.1 = (bf16[64,2176]{1,0:T(8,128)(2,1)S(1)}, s32[72]{0:T(128)S(1)}) custom-call(s32[2]{0:T(128)S(1)} %pad_add_fusion.place_ref, bf16[4,16,2048]{2,1,0:T(8,128)(2,1)S(1)} %bitcast.18, s32[4,16]{1,0:T(4,128)S(1)} %broadcast_select_fusion.rest_0_, bf16[4096,128]{1,0:T(8,128)(2,1)S(1)} %copy-done.1, bf16[4096,128]{1,0:T(8,128)(2,1)S(1)} %copy-done.2, ...), custom_call_target="tpu_custom_call" | custom-call | flops 536870912 | bytes 8388608 | tf_op jit(solution)/shard_map/attend_own/pallas_call | solution.py:274
  34.9 0.0 copy-start.4
  34.9 0.7 copy-done.4
  35.6 7.0 %all-to-all-done.1 = bf16[4,64,2048]{2,1,0:T(8,128)(2,1)S(1)} async-done(((bf16[4,64,2048]{2,1,0:T(8,128)(2,1)}), bf16[4,64,2048]{2,1,0:T(8,128)(2,1)S(1)}, u32[]{:S(2)}, u32[]{:S(2)}) %all-to-all-start.1) | async-done | bytes 1048608 | tf_op jit(solution)/shard_map/all_to_all | solution.py:57
  42.5 9.1 %attend_rest.1 = bf16[4,64,2176]{2,1,0:T(8,128)(2,1)S(1)} custom-call(s32[2]{0:T(128)S(1)} %pad_add_fusion.place_ref, bf16[4,4,16,2048]{3,2,1,0:T(8,128)(2,1)S(1)} %bitcast.16, s32[72]{0:T(128)S(1)} %get-tuple-element.10.rest_0_, bf16[4096,128]{1,0:T(8,128)(2,1)S(1)} %copy-done.1, bf16[4096,128]{1,0:T(8,128)(2,1)S(1)} %copy-done.2, ...), custom_call_target="tpu_custom_call" | custom-call | flops 1610612736 | bytes 8388608 | tf_op jit(solution)/shard_map/attend_rest/pallas_call | solution.py:288
  51.6 0.0 copy-start.5
  51.6 15.3 %all_to_all.35.in_ref = bf16[4,64,2176]{2,1,0:T(8,128)(2,1)S(1)} all-to-all(bf16[4,64,2176]{2,1,0:T(8,128)(2,1)S(1)} %attend_rest.1), channel_id=1, replica_groups={{0,16,32,48},{8,24,40,56},{64,80,96,112},{72,88,104,120},{128,144,160,1..., dimensions={0} | all-to-all | bytes 2228224 | tf_op jit(solution)/shard_map/all_to_all | solution.py:57
  67.0 0.0 copy-done.5
  67.0 1.3 merge.1
  68.2 19.4 %all_to_all.36 = bf16[8,8,2176]{2,1,0:T(8,128)(2,1)S(1)} all-to-all(bf16[8,8,2176]{2,1,0:T(8,128)(2,1)S(1)} %bitcast.19), channel_id=1, replica_groups={{0,64,128,192,256,320,384,448},{8,72,136,200,264,328,392,456},{16,80,14..., dimensions={0} | all-to-all | bytes 557056 | tf_op jit(solution)/shard_map/all_to_all | solution.py:57
  87.6 0.4 shard_map.64
  88.0 11.1 %all_to_all.37 = bf16[4,8,2048]{2,1,0:T(8,128)(2,1)S(1)} all-to-all(bf16[4,8,2048]{2,1,0:T(8,128)(2,1)S(1)} %bitcast.22), channel_id=1, replica_groups={{0,128,256,384},{72,200,328,456},{16,144,272,400},{88,216,344,472},{32,..., dimensions={0} | all-to-all | bytes 262144 | tf_op jit(solution)/shard_map/all_to_all | solution.py:57
  99.2 1.1 broadcast_in_dim.26
  100.3 0.0 copy-start.3
  100.3 3.7 %all-to-all-start.5 = ((bf16[8,32,2048]{2,1,0:T(8,128)(2,1)}), bf16[8,32,2048]{2,1,0:T(8,128)(2,1)S(1)}, u32[]{:S(2)}, u32[]{:S(2)}) async-start(bf16[8,32,2048]{2,1,0:T(8,128)(2,1)} %broadcast_in_dim.26), calls=%async_computation.5 | async-start | bytes 2097152 | tf_op jit(solution)/shard_map/all_to_all | solution.py:57
  104.0 0.0 copy-done.3
  104.0 1.9 %collective-permute-start.2 = (bf16[2048,256]{1,0:T(8,128)(2,1)S(1)}, bf16[2048,256]{1,0:T(8,128)(2,1)S(1)}, u32[]{:S(2)}, u32[]{:S(2)}) collective-permute-start(bf16[2048,256]{1,0:T(8,128)(2,1)S(1)} %copy-done.3), channel_id=1, source_target_pairs={{0,8},{8,0},{16,24},{24,16},{32,40},{40,32},{48,56},{56,48},{64,72... | collective-permute-start | bytes 3145736 | tf_op jit(solution)/shard_map/ppermute | solution.py:423
  105.9 2.6 %collective-permute-done.2.w1_ref = bf16[2048,256]{1,0:T(8,128)(2,1)S(1)} collective-permute-done((bf16[2048,256]{1,0:T(8,128)(2,1)S(1)}, bf16[2048,256]{1,0:T(8,128)(2,1)S(1)}, u32[]{:S(2)}, u32[]{:S(2)}) %collective-permute-start.2) | collective-permute-done | bytes 1048608 | tf_op jit(solution)/shard_map/ppermute | solution.py:423
  108.5 5.9 %all-to-all-done.5.a_ref = bf16[8,32,2048]{2,1,0:T(8,128)(2,1)S(1)} async-done(((bf16[8,32,2048]{2,1,0:T(8,128)(2,1)}), bf16[8,32,2048]{2,1,0:T(8,128)(2,1)S(1)}, u32[]{:S(2)}, u32[]{:S(2)}) %all-to-all-start.5) | async-done | bytes 1048608 | tf_op jit(solution)/shard_map/all_to_all | solution.py:57
  114.5 0.7 shard_map.65
  115.2 16.3 %all_to_all.38 = bf16[16,32,256]{2,1,0:T(8,128)(2,1)S(1)} all-to-all(bf16[16,32,256]{2,1,0:T(8,128)(2,1)S(1)} %bitcast.21), channel_id=1, replica_groups={{0,1,2,3,4,5,6,7,8,9,10,11,12,13,14,15},{16,17,18,19,20,21,22,23,24,25,..., dimensions={0} | all-to-all | bytes 524288 | tf_op jit(solution)/shard_map/all_to_all | solution.py:57
  131.6 0.6 copy.8
  (6 shorter events, 0.1 us)
Async XLA Ops:
  0.0 29.3 %copy-start = (s32[8,4,64]{2,1,0:T(4,128)S(1)}, s32[8,4,64]{2,1,0:T(4,128)}, u32[]{:S(2)}) copy-start(s32[8,4,64]{2,1,0:T(4,128)} %param.10) | copy-start | bytes 24580
  1.5 22.2 %all-to-all-start = ((bf16[8,8,2048]{2,1,0:T(8,128)(2,1)}), bf16[8,8,2048]{2,1,0:T(8,128)(2,1)S(1)}, u32[]{:S(2)}, u32[]{:S(2)}) async-start(bf16[8,8,2048]{2,1,0:T(8,128)(2,1)} %broadcast_in_dim.10), calls=%async_computation | async-start | bytes 524288 | tf_op jit(solution)/shard_map/all_to_all | solution.py:57
  11.8 17.7 %collective-permute-start = (bf16[4096,128]{1,0:T(8,128)(2,1)}, bf16[4096,128]{1,0:T(8,128)(2,1)}, u32[]{:S(2)}, u32[]{:S(2)}) collective-permute-start(bf16[4096,128]{1,0:T(8,128)(2,1)} %rest_1_.3), channel_id=1, source_target_pairs={{0,8},{8,0},{16,24},{24,16},{32,40},{40,32},{48,56},{56,48},{64,72... | collective-permute-start | bytes 3145736 | tf_op jit(solution)/shard_map/ppermute | solution.py:414
  13.7 15.8 %collective-permute-start.1 = (bf16[4096,128]{1,0:T(8,128)(2,1)}, bf16[4096,128]{1,0:T(8,128)(2,1)}, u32[]{:S(2)}, u32[]{:S(2)}) collective-permute-start(bf16[4096,128]{1,0:T(8,128)(2,1)} %rest_2_.3), channel_id=1, source_target_pairs={{0,8},{8,0},{16,24},{24,16},{32,40},{40,32},{48,56},{56,48},{64,72... | collective-permute-start | bytes 3145736 | tf_op jit(solution)/shard_map/ppermute | solution.py:415
  24.8 4.8 %copy-start.1 = (bf16[4096,128]{1,0:T(8,128)(2,1)S(1)}, bf16[4096,128]{1,0:T(8,128)(2,1)}, u32[]{:S(2)}) copy-start(bf16[4096,128]{1,0:T(8,128)(2,1)} %rest_1_.3) | copy-start | bytes 3145732
  24.8 4.8 %copy-start.2 = (bf16[4096,128]{1,0:T(8,128)(2,1)S(1)}, bf16[4096,128]{1,0:T(8,128)(2,1)}, u32[]{:S(2)}) copy-start(bf16[4096,128]{1,0:T(8,128)(2,1)} %rest_2_.3) | copy-start | bytes 3145732
  24.8 17.7 %all-to-all-start.1 = ((bf16[4,64,2048]{2,1,0:T(8,128)(2,1)}), bf16[4,64,2048]{2,1,0:T(8,128)(2,1)S(1)}, u32[]{:S(2)}, u32[]{:S(2)}) async-start(bf16[4,64,2048]{2,1,0:T(8,128)(2,1)} %broadcast_in_dim.24), calls=%async_computation.1 | async-start | bytes 2097152 | tf_op jit(solution)/shard_map/all_to_all | solution.py:57
  34.9 0.7 copy-start.4
  51.6 15.3 %copy-start.5 = (bf16[64,2176]{1,0:T(8,128)(2,1)S(1)}, bf16[64,2176]{1,0:T(8,128)(2,1)}, u32[]{:S(2)}) copy-start(bf16[64,2176]{1,0:T(8,128)(2,1)} %copy-done.4) | copy-start | bytes 835588
  100.3 3.7 %copy-start.3 = (bf16[2048,256]{1,0:T(8,128)(2,1)S(1)}, bf16[2048,256]{1,0:T(8,128)(2,1)}, u32[]{:S(2)}) copy-start(bf16[2048,256]{1,0:T(8,128)(2,1)} %w0_ref) | copy-start | bytes 3145732
  100.3 14.2 %all-to-all-start.5 = ((bf16[8,32,2048]{2,1,0:T(8,128)(2,1)}), bf16[8,32,2048]{2,1,0:T(8,128)(2,1)S(1)}, u32[]{:S(2)}, u32[]{:S(2)}) async-start(bf16[8,32,2048]{2,1,0:T(8,128)(2,1)} %broadcast_in_dim.26), calls=%async_computation.5 | async-start | bytes 2097152 | tf_op jit(solution)/shard_map/all_to_all | solution.py:57
  104.0 4.6 %collective-permute-start.2 = (bf16[2048,256]{1,0:T(8,128)(2,1)S(1)}, bf16[2048,256]{1,0:T(8,128)(2,1)S(1)}, u32[]{:S(2)}, u32[]{:S(2)}) collective-permute-start(bf16[2048,256]{1,0:T(8,128)(2,1)S(1)} %copy-done.3), channel_id=1, source_target_pairs={{0,8},{8,0},{16,24},{24,16},{32,40},{40,32},{48,56},{56,48},{64,72... | collective-permute-start | bytes 3145736 | tf_op jit(solution)/shard_map/ppermute | solution.py:423

commit v6 on v4

--- a/solution.py
+++ b/solution.py
@@ -46,7 +46,7 @@
     for c in range(2)
 ]
 YC_GROUPS = [
-    [place(z, x, c) * YN + y for c in range(2) for y in range(YN)]
+    [place(z, x, c) * YN + (y + c * (YN // 2)) % YN for c in range(2) for y in range(YN)]
     for z in range(ZN)
     for x in range(XN)
 ]
@@ -369,7 +369,7 @@
             pair, low = w // 2, w % 2
             starts = [((low * XN + x) * (ZN // 2) + pair) * ROWS for x in range(XN)]
             chunk = jnp.concatenate([result[start : start + ROWS] for start in starts], axis=0)
-            out_ref[target, lax.rem(w + core, ZN)] = chunk.astype(BF16)
+            out_ref[target, lax.rem(w + core + target * (YN // 2), ZN)] = chunk.astype(BF16)
 
 
 def project(core, rows, w0, w1):

time: 132 us -> 131 us (level)
  transfers between devices with their start and end apart: 6 -> 6, of which waited for: 4 -> 4; matrix products, arithmetic and copies ran while one was open for 2% -> 2% of each run, Pallas kernels for 4% -> 3%
where the time goes in v6:
time: 131 us; the launch traced here: 130 us
  blocking collectives  64.1 us (49%)
  starting transfers between devices  24.7 us (19%)
  waiting for transfers between devices  23 us (18%)
  Pallas kernels  11.9 us (9%)
  local copies, waits for them, and re-layouts  6.01 us (5%)
    all_to_all x4, blocking collectives, exchange(): lax.all_to_all(blocks, axis, split_axis=0, concat_axis=0, tiled=True, axi...  64.1 us
    all_to_all x3, waiting for transfers between devices, exchange(): lax.all_to_all(blocks, axis, split_axis=0, concat_axis=0, tiled=True, axi...  20.4 us
    all_to_all x3, starting transfers between devices, exchange(): lax.all_to_all(blocks, axis, split_axis=0, concat_axis=0, tiled=True, axi...  18.4 us
    pallas_call x1, Pallas kernels, attend_rest(): pl.pallas_call(functools.partial(attend_kernel, False), name='attend_rest...  5.28 us
    pallas_call x1, Pallas kernels, attend_own(): pl.pallas_call(functools.partial(attend_kernel, True), name='attend_own',...  4.32 us
    broadcast_in_dim x3, local copies, waits for them, and re-layouts, spread(): jnp.broadcast_to(rows[None], (count,) + rows.shape)  3.69 us
    ppermute x1, waiting for transfers between devices, body(): other_weight = lax.ppermute(out_weight, 'ctx', CORE_SWAP)  2.63 us
  transfers between devices with their start and end apart: 6, of which 4 were waited for; matrix products, arithmetic and copies ran while one was open for 2% of the time, Pallas kernels for 3%

profile of v6, /device:TPU:8, one launch (start us, length us, event | category | flops | bytes accessed | tf_op | source)
XLA Modules:
  0.0 130.3 jit_solution(16173145833979676093)
XLA Ops:
  0.0 0.0 copy-start
  0.0 1.5 %broadcast_in_dim.10 = bf16[8,8,2048]{2,1,0:T(8,128)(2,1)} broadcast(bf16[8,2048]{1,0:T(8,128)(2,1)} %param.6), dimensions={1,2} | broadcast | bytes 294912 | tf_op jit(solution)/shard_map/broadcast_in_dim | solution.py:64
  1.5 10.3 %all-to-all-start = ((bf16[8,8,2048]{2,1,0:T(8,128)(2,1)}), bf16[8,8,2048]{2,1,0:T(8,128)(2,1)S(1)}, u32[]{:S(2)}, u32[]{:S(2)}) async-start(bf16[8,8,2048]{2,1,0:T(8,128)(2,1)} %broadcast_in_dim.10), calls=%async_computation | async-start | bytes 524288 | tf_op jit(solution)/shard_map/all_to_all | solution.py:57
  11.8 1.9 %collective-permute-start = (bf16[4096,128]{1,0:T(8,128)(2,1)}, bf16[4096,128]{1,0:T(8,128)(2,1)}, u32[]{:S(2)}, u32[]{:S(2)}) collective-permute-start(bf16[4096,128]{1,0:T(8,128)(2,1)} %rest_1_.3), channel_id=1, source_target_pairs={{0,8},{8,0},{16,24},{24,16},{32,40},{40,32},{48,56},{56,48},{64,72... | collective-permute-start | bytes 3145736 | tf_op jit(solution)/shard_map/ppermute | solution.py:401
  13.7 2.4 %collective-permute-start.1 = (bf16[4096,128]{1,0:T(8,128)(2,1)}, bf16[4096,128]{1,0:T(8,128)(2,1)}, u32[]{:S(2)}, u32[]{:S(2)}) collective-permute-start(bf16[4096,128]{1,0:T(8,128)(2,1)} %rest_2_.3), channel_id=1, source_target_pairs={{0,8},{8,0},{16,24},{24,16},{32,40},{40,32},{48,56},{56,48},{64,72... | collective-permute-start | bytes 3145736 | tf_op jit(solution)/shard_map/ppermute | solution.py:402
  16.2 0.8 dynamic_slice.8
  16.9 0.1 reshape.43
  17.1 0.1 eq.35
  17.1 6.5 %all-to-all-done = bf16[8,8,2048]{2,1,0:T(8,128)(2,1)S(1)} async-done(((bf16[8,8,2048]{2,1,0:T(8,128)(2,1)}), bf16[8,8,2048]{2,1,0:T(8,128)(2,1)S(1)}, u32[]{:S(2)}, u32[]{:S(2)}) %all-to-all-start) | async-done | bytes 262176 | tf_op jit(solution)/shard_map/all_to_all | solution.py:57
  23.7 1.1 broadcast_in_dim.24
  24.8 0.0 copy-start.1
  24.8 0.0 copy-start.2
  24.8 4.4 %all-to-all-start.1 = ((bf16[4,64,2048]{2,1,0:T(8,128)(2,1)}), bf16[4,64,2048]{2,1,0:T(8,128)(2,1)S(1)}, u32[]{:S(2)}, u32[]{:S(2)}) async-start(bf16[4,64,2048]{2,1,0:T(8,128)(2,1)} %broadcast_in_dim.24), calls=%async_computation.1 | async-start | bytes 2097152 | tf_op jit(solution)/shard_map/all_to_all | solution.py:57
  29.2 0.1 pad_add_fusion.place_ref
  29.3 0.0 copy-done
  29.3 0.2 compare_reduce_fusion
  29.5 0.0 collective-permute-done.rest_3_
  29.6 0.0 collective-permute-done.1.rest_4_
  29.6 0.0 copy-done.1
  29.6 0.0 copy-done.2
  29.6 4.3 %attend_own.1 = (bf16[64,2176]{1,0:T(8,128)(2,1)S(1)}, s32[72]{0:T(128)S(1)}) custom-call(s32[2]{0:T(128)S(1)} %pad_add_fusion.place_ref, bf16[4,16,2048]{2,1,0:T(8,128)(2,1)S(1)} %bitcast.18, s32[4,16]{1,0:T(4,128)S(1)} %broadcast_select_fusion.rest_0_, bf16[4096,128]{1,0:T(8,128)(2,1)S(1)} %copy-done.1, bf16[4096,128]{1,0:T(8,128)(2,1)S(1)} %copy-done.2, ...), custom_call_target="tpu_custom_call" | custom-call | flops 536870912 | bytes 8388608 | tf_op jit(solution)/shard_map/attend_own/pallas_call | solution.py:262
  33.9 0.0 copy-start.4
  33.9 0.7 copy-done.4
  34.6 7.9 %all-to-all-done.1 = bf16[4,64,2048]{2,1,0:T(8,128)(2,1)S(1)} async-done(((bf16[4,64,2048]{2,1,0:T(8,128)(2,1)}), bf16[4,64,2048]{2,1,0:T(8,128)(2,1)S(1)}, u32[]{:S(2)}, u32[]{:S(2)}) %all-to-all-start.1) | async-done | bytes 1048608 | tf_op jit(solution)/shard_map/all_to_all | solution.py:57
  42.5 5.3 %attend_rest.1 = bf16[4,64,2176]{2,1,0:T(8,128)(2,1)S(1)} custom-call(s32[2]{0:T(128)S(1)} %pad_add_fusion.place_ref, bf16[4,4,16,2048]{3,2,1,0:T(8,128)(2,1)S(1)} %bitcast.16, s32[72]{0:T(128)S(1)} %get-tuple-element.10.rest_0_, bf16[4096,128]{1,0:T(8,128)(2,1)S(1)} %copy-done.1, bf16[4096,128]{1,0:T(8,128)(2,1)S(1)} %copy-done.2, ...), custom_call_target="tpu_custom_call" | custom-call | flops 1610612736 | bytes 8388608 | tf_op jit(solution)/shard_map/attend_rest/pallas_call | solution.py:275
  47.8 0.0 copy-start.5
  47.8 17.1 %all_to_all.35.in_ref = bf16[4,64,2176]{2,1,0:T(8,128)(2,1)S(1)} all-to-all(bf16[4,64,2176]{2,1,0:T(8,128)(2,1)S(1)} %attend_rest.1), channel_id=1, replica_groups={{0,16,32,48},{8,24,40,56},{64,80,96,112},{72,88,104,120},{128,144,160,1..., dimensions={0} | all-to-all | bytes 2228224 | tf_op jit(solution)/shard_map/all_to_all | solution.py:57
  64.9 0.0 copy-done.5
  64.9 1.3 merge.1
  66.2 17.7 %all_to_all.36 = bf16[8,8,2176]{2,1,0:T(8,128)(2,1)S(1)} all-to-all(bf16[8,8,2176]{2,1,0:T(8,128)(2,1)S(1)} %bitcast.19), channel_id=1, replica_groups={{0,64,128,192,256,320,384,448},{8,72,136,200,264,328,392,456},{16,80,14..., dimensions={0} | all-to-all | bytes 557056 | tf_op jit(solution)/shard_map/all_to_all | solution.py:57
  83.9 0.4 shard_map.64
  84.3 11.2 %all_to_all.37 = bf16[4,8,2048]{2,1,0:T(8,128)(2,1)S(1)} all-to-all(bf16[4,8,2048]{2,1,0:T(8,128)(2,1)S(1)} %bitcast.22), channel_id=1, replica_groups={{0,128,256,384},{72,200,328,456},{16,144,272,400},{88,216,344,472},{32,..., dimensions={0} | all-to-all | bytes 262144 | tf_op jit(solution)/shard_map/all_to_all | solution.py:57
  95.5 1.1 broadcast_in_dim.26
  96.6 0.0 copy-start.3
  96.6 3.7 %all-to-all-start.5 = ((bf16[8,32,2048]{2,1,0:T(8,128)(2,1)}), bf16[8,32,2048]{2,1,0:T(8,128)(2,1)S(1)}, u32[]{:S(2)}, u32[]{:S(2)}) async-start(bf16[8,32,2048]{2,1,0:T(8,128)(2,1)} %broadcast_in_dim.26), calls=%async_computation.5 | async-start | bytes 2097152 | tf_op jit(solution)/shard_map/all_to_all | solution.py:57
  100.3 0.0 copy-done.3
  100.4 1.9 %collective-permute-start.2 = (bf16[2048,256]{1,0:T(8,128)(2,1)S(1)}, bf16[2048,256]{1,0:T(8,128)(2,1)S(1)}, u32[]{:S(2)}, u32[]{:S(2)}) collective-permute-start(bf16[2048,256]{1,0:T(8,128)(2,1)S(1)} %copy-done.3), channel_id=1, source_target_pairs={{0,8},{8,0},{16,24},{24,16},{32,40},{40,32},{48,56},{56,48},{64,72... | collective-permute-start | bytes 3145736 | tf_op jit(solution)/shard_map/ppermute | solution.py:410
  102.3 2.6 %collective-permute-done.2.w1_ref = bf16[2048,256]{1,0:T(8,128)(2,1)S(1)} collective-permute-done((bf16[2048,256]{1,0:T(8,128)(2,1)S(1)}, bf16[2048,256]{1,0:T(8,128)(2,1)S(1)}, u32[]{:S(2)}, u32[]{:S(2)}) %collective-permute-start.2) | collective-permute-done | bytes 1048608 | tf_op jit(solution)/shard_map/ppermute | solution.py:410
  104.9 5.9 %all-to-all-done.5.a_ref = bf16[8,32,2048]{2,1,0:T(8,128)(2,1)S(1)} async-done(((bf16[8,32,2048]{2,1,0:T(8,128)(2,1)}), bf16[8,32,2048]{2,1,0:T(8,128)(2,1)S(1)}, u32[]{:S(2)}, u32[]{:S(2)}) %all-to-all-start.5) | async-done | bytes 1048608 | tf_op jit(solution)/shard_map/all_to_all | solution.py:57
  110.9 0.7 shard_map.65
  111.6 18.1 %all_to_all.38 = bf16[16,32,256]{2,1,0:T(8,128)(2,1)S(1)} all-to-all(bf16[16,32,256]{2,1,0:T(8,128)(2,1)S(1)} %bitcast.21), channel_id=1, replica_groups={{0,1,2,3,4,5,6,7,12,13,14,15,8,9,10,11},{16,17,18,19,20,21,22,23,28,29,..., dimensions={0} | all-to-all | bytes 524288 | tf_op jit(solution)/shard_map/all_to_all | solution.py:57
  129.7 0.6 copy.8
  (6 shorter events, 0.1 us)
Async XLA Ops:
  0.0 29.3 %copy-start = (s32[8,4,64]{2,1,0:T(4,128)S(1)}, s32[8,4,64]{2,1,0:T(4,128)}, u32[]{:S(2)}) copy-start(s32[8,4,64]{2,1,0:T(4,128)} %param.10) | copy-start | bytes 24580
  1.5 22.2 %all-to-all-start = ((bf16[8,8,2048]{2,1,0:T(8,128)(2,1)}), bf16[8,8,2048]{2,1,0:T(8,128)(2,1)S(1)}, u32[]{:S(2)}, u32[]{:S(2)}) async-start(bf16[8,8,2048]{2,1,0:T(8,128)(2,1)} %broadcast_in_dim.10), calls=%async_computation | async-start | bytes 524288 | tf_op jit(solution)/shard_map/all_to_all | solution.py:57
  11.8 17.7 %collective-permute-start = (bf16[4096,128]{1,0:T(8,128)(2,1)}, bf16[4096,128]{1,0:T(8,128)(2,1)}, u32[]{:S(2)}, u32[]{:S(2)}) collective-permute-start(bf16[4096,128]{1,0:T(8,128)(2,1)} %rest_1_.3), channel_id=1, source_target_pairs={{0,8},{8,0},{16,24},{24,16},{32,40},{40,32},{48,56},{56,48},{64,72... | collective-permute-start | bytes 3145736 | tf_op jit(solution)/shard_map/ppermute | solution.py:401
  13.7 15.8 %collective-permute-start.1 = (bf16[4096,128]{1,0:T(8,128)(2,1)}, bf16[4096,128]{1,0:T(8,128)(2,1)}, u32[]{:S(2)}, u32[]{:S(2)}) collective-permute-start(bf16[4096,128]{1,0:T(8,128)(2,1)} %rest_2_.3), channel_id=1, source_target_pairs={{0,8},{8,0},{16,24},{24,16},{32,40},{40,32},{48,56},{56,48},{64,72... | collective-permute-start | bytes 3145736 | tf_op jit(solution)/shard_map/ppermute | solution.py:402
  24.8 4.8 %copy-start.1 = (bf16[4096,128]{1,0:T(8,128)(2,1)S(1)}, bf16[4096,128]{1,0:T(8,128)(2,1)}, u32[]{:S(2)}) copy-start(bf16[4096,128]{1,0:T(8,128)(2,1)} %rest_1_.3) | copy-start | bytes 3145732
  24.8 4.8 %copy-start.2 = (bf16[4096,128]{1,0:T(8,128)(2,1)S(1)}, bf16[4096,128]{1,0:T(8,128)(2,1)}, u32[]{:S(2)}) copy-start(bf16[4096,128]{1,0:T(8,128)(2,1)} %rest_2_.3) | copy-start | bytes 3145732
  24.8 17.7 %all-to-all-start.1 = ((bf16[4,64,2048]{2,1,0:T(8,128)(2,1)}), bf16[4,64,2048]{2,1,0:T(8,128)(2,1)S(1)}, u32[]{:S(2)}, u32[]{:S(2)}) async-start(bf16[4,64,2048]{2,1,0:T(8,128)(2,1)} %broadcast_in_dim.24), calls=%async_computation.1 | async-start | bytes 2097152 | tf_op jit(solution)/shard_map/all_to_all | solution.py:57
  33.9 0.7 copy-start.4
  47.8 17.1 %copy-start.5 = (bf16[64,2176]{1,0:T(8,128)(2,1)S(1)}, bf16[64,2176]{1,0:T(8,128)(2,1)}, u32[]{:S(2)}) copy-start(bf16[64,2176]{1,0:T(8,128)(2,1)} %copy-done.4) | copy-start | bytes 835588
  96.6 3.7 %copy-start.3 = (bf16[2048,256]{1,0:T(8,128)(2,1)S(1)}, bf16[2048,256]{1,0:T(8,128)(2,1)}, u32[]{:S(2)}) copy-start(bf16[2048,256]{1,0:T(8,128)(2,1)} %w0_ref) | copy-start | bytes 3145732
  96.6 14.2 %all-to-all-start.5 = ((bf16[8,32,2048]{2,1,0:T(8,128)(2,1)}), bf16[8,32,2048]{2,1,0:T(8,128)(2,1)S(1)}, u32[]{:S(2)}, u32[]{:S(2)}) async-start(bf16[8,32,2048]{2,1,0:T(8,128)(2,1)} %broadcast_in_dim.26), calls=%async_computation.5 | async-start | bytes 2097152 | tf_op jit(solution)/shard_map/all_to_all | solution.py:57
  100.4 4.6 %collective-permute-start.2 = (bf16[2048,256]{1,0:T(8,128)(2,1)S(1)}, bf16[2048,256]{1,0:T(8,128)(2,1)S(1)}, u32[]{:S(2)}, u32[]{:S(2)}) collective-permute-start(bf16[2048,256]{1,0:T(8,128)(2,1)S(1)} %copy-done.3), channel_id=1, source_target_pairs={{0,8},{8,0},{16,24},{24,16},{32,40},{40,32},{48,56},{56,48},{64,72... | collective-permute-start | bytes 3145736 | tf_op jit(solution)/shard_map/ppermute | solution.py:410
